TPU v7x, 32 devices: a whole 2x2x4 slice. The times are simulated.
32 devices in a mesh: section: 2 (over y), dp: 16 (over z, x, core).
Axes of the slice: x: 2, y: 2, z: 4, core: 2. Of those that a mesh axis runs over, the one named last changes fastest.
Arguments:
- inputs: bfloat16 [2, 32, 1024, 512], P('section', 'dp'), may hold values from -6 to 6
- cotangent: bfloat16 [2, 32, 1024, 512], P('section', 'dp'), may hold values from -6 to 6
- lengths: int32 [32, 8], P('dp'), may hold values from 1 to 256, 1024 in all within a row
- norm1_gain: float32 [2, 512], P('section'), may hold values from 0.25 to 1.75
- norm1_bias: float32 [2, 512], P('section'), may hold values from -1 to 1
- weight_qkv: bfloat16 [2, 512, 1536], P('section'), may hold values from -0.25 to 0.25
- weight_out: bfloat16 [2, 512, 512], P('section'), may hold values from -0.75 to 0.75
- bias_out: float32 [2, 512], P('section'), may hold values from -1 to 1
- norm2_gain: float32 [2, 512], P('section'), may hold values from 0.25 to 1.75
- norm2_bias: float32 [2, 512], P('section'), may hold values from -1 to 1
- weight_up: bfloat16 [2, 512, 2048], P('section'), may hold values from -0.25 to 0.25
- bias_up: float32 [2, 2048], P('section'), may hold values from -1 to 1
- weight_down: bfloat16 [2, 2048, 512], P('section'), may hold values from -0.125 to 0.125
- bias_down: float32 [2, 512], P('section'), may hold values from -1 to 1
Outputs:
- outputs: bfloat16 [2, 32, 1024, 512], P('section', 'dp')
- input_grad: float32 [2, 32, 1024, 512], P('section', 'dp')
- grad_norm1_gain: float32 [2, 512], P('section')
- grad_norm1_bias: float32 [2, 512], P('section')
- grad_weight_qkv: float32 [2, 512, 1536], P('section')
- grad_weight_out: float32 [2, 512, 512], P('section')
- grad_bias_out: float32 [2, 512], P('section')
- grad_norm2_gain: float32 [2, 512], P('section')
- grad_norm2_bias: float32 [2, 512], P('section')
- grad_weight_up: float32 [2, 512, 2048], P('section')
- grad_bias_up: float32 [2, 2048], P('section')
- grad_weight_down: float32 [2, 2048, 512], P('section')
- grad_bias_down: float32 [2, 512], P('section')
Inputs may be any that keep to these rules, and one draw needn't show every extreme that they name: Each row of lengths holds 8 span lengths that sum to 1024; the last span of each row is its padded tail.
All inputs are finite; a program needn't handle non-finite values.
Results may differ from a plain program's by a relative error of at most 0.014.
Values may be sent and summed in bfloat16 or wider, within the bound.
A program may use at most 448 MiB of HBM per device.

v0:
```python
import jax
import jax.numpy as jnp
from jax import lax
from jax.sharding import PartitionSpec as P

HEADS = 8
MICRO = 2


EPSILON = 1e-05
SCORE_SCALE = 0.125
MASKED_SCORE = -1e30


def from_behind(block, axis, distance):
    devices = range(lax.axis_size(axis))
    route = [(i - distance, i) for i in devices if i - distance in devices]
    return lax.ppermute(block, axis, route)


def layer_norm(hidden, norm_gain, norm_bias):
    centred = hidden - jnp.mean(hidden, -1, keepdims=True)
    scaled = centred * lax.rsqrt(jnp.mean(centred * centred, -1, keepdims=True) + EPSILON)
    return scaled * norm_gain + norm_bias


def gelu_smooth(value):
    return jax.nn.gelu(value, approximate=True)


def segment_ids(lengths, length):
    ends = jnp.cumsum(lengths, -1)
    position = jnp.arange(length, dtype=jnp.int32)
    return jnp.sum(
        (position[None, :, None] >= ends[:, None, :]).astype(jnp.int32), -1, dtype=jnp.int32
    )


def split_heads(projected, head_count):
    row_count, length, triple = projected.shape
    width_all = triple // 3
    shape_four = (row_count, length, head_count, width_all // head_count)
    return (
        projected[..., :width_all].reshape(shape_four),
        projected[..., width_all : 2 * width_all].reshape(shape_four),
        projected[..., 2 * width_all :].reshape(shape_four),
    )


def block_scores(queries, keys_all, query_segments, key_segments):
    scores = (
        jnp.einsum("bqhd,bkhd->bhqk", queries, keys_all, preferred_element_type=jnp.float32)
        * SCORE_SCALE
    )
    allowed = query_segments[:, None, :, None] == key_segments[:, None, None, :]
    return jnp.where(allowed, scores, MASKED_SCORE)


def attend_forward(projected, segments, head_count):
    row_count, length, triple = projected.shape
    queries, keys_all, values_all = split_heads(projected, head_count)
    block_rows = min(512, length)
    mixed_parts = []
    total_parts = []
    for begin_row in range(0, length, block_rows):
        end_row = begin_row + block_rows
        scores = block_scores(
            queries[:, begin_row:end_row], keys_all, segments[:, begin_row:end_row], segments
        )
        highest = jnp.max(scores, -1, keepdims=True)
        raised = jnp.exp(scores - highest)
        total = jnp.sum(raised, -1, keepdims=True)
        probs = (raised / total).astype(jnp.bfloat16)
        log_total = highest + jnp.log(total)
        mixed = jnp.einsum("bhqk,bkhd->bqhd", probs, values_all, preferred_element_type=jnp.float32)
        mixed_parts.append(mixed.reshape(row_count, block_rows, triple // 3).astype(jnp.bfloat16))
        total_parts.append(log_total)
    return (jnp.concatenate(mixed_parts, 1), jnp.concatenate(total_parts, 2))


def attend_backward(projected, segments, log_total, mixed_grad, head_count):
    row_count, length, triple = projected.shape
    width_all = triple // 3
    queries, keys_all, values_all = split_heads(projected, head_count)
    out_grad = mixed_grad.reshape(queries.shape)
    block_rows = min(512, length)
    key_grad = jnp.zeros(queries.shape, jnp.float32)
    value_grad = jnp.zeros(queries.shape, jnp.float32)
    query_parts = []
    for begin_row in range(0, length, block_rows):
        end_row = begin_row + block_rows
        block_queries = queries[:, begin_row:end_row]
        block_out = out_grad[:, begin_row:end_row]
        scores = block_scores(block_queries, keys_all, segments[:, begin_row:end_row], segments)
        probs = jnp.exp(scores - log_total[:, :, begin_row:end_row])
        prob_grad = jnp.einsum(
            "bqhd,bkhd->bhqk", block_out, values_all, preferred_element_type=jnp.float32
        )
        inner = jnp.sum(prob_grad * probs, -1, keepdims=True)
        score_grad = (probs * (prob_grad - inner)).astype(jnp.bfloat16)
        query_parts.append(
            jnp.einsum("bhqk,bkhd->bqhd", score_grad, keys_all, preferred_element_type=jnp.float32)
            * SCORE_SCALE
        )
        key_grad = (
            key_grad
            + jnp.einsum(
                "bhqk,bqhd->bkhd", score_grad, block_queries, preferred_element_type=jnp.float32
            )
            * SCORE_SCALE
        )
        value_grad = value_grad + jnp.einsum(
            "bhqk,bqhd->bkhd",
            probs.astype(jnp.bfloat16),
            block_out,
            preferred_element_type=jnp.float32,
        )
    flat_shape = (row_count, length, width_all)
    joined = jnp.concatenate(
        [
            jnp.concatenate(query_parts, 1).reshape(flat_shape),
            key_grad.reshape(flat_shape),
            value_grad.reshape(flat_shape),
        ],
        -1,
    )
    return joined.astype(jnp.bfloat16)


def layer_forward(params, hidden, segments):
    (
        norm1_gain,
        norm1_bias,
        weight_qkv,
        weight_out,
        bias_out,
        norm2_gain,
        norm2_bias,
        weight_up,
        bias_up,
        weight_down,
        bias_down,
    ) = params
    first_low = layer_norm(hidden, norm1_gain, norm1_bias).astype(jnp.bfloat16)
    projected = jnp.einsum(
        "bld,de->ble", first_low, weight_qkv, preferred_element_type=jnp.float32
    ).astype(jnp.bfloat16)
    mixed, log_total = attend_forward(projected, segments, HEADS)
    attended = (
        hidden
        + jnp.einsum("bld,de->ble", mixed, weight_out, preferred_element_type=jnp.float32)
        + bias_out
    )
    second_low = layer_norm(attended, norm2_gain, norm2_bias).astype(jnp.bfloat16)
    upward = (
        jnp.einsum("bld,df->blf", second_low, weight_up, preferred_element_type=jnp.float32)
        + bias_up
    )
    gelu_low = gelu_smooth(upward).astype(jnp.bfloat16)
    output = (
        attended
        + jnp.einsum("blf,fd->bld", gelu_low, weight_down, preferred_element_type=jnp.float32)
        + bias_down
    )
    return (
        output,
        (first_low, projected, mixed, log_total, attended, second_low, upward, gelu_low),
    )


def layer_backward(params, hidden, segments, saved, grad_out):
    (
        norm1_gain,
        norm1_bias,
        weight_qkv,
        weight_out,
        bias_out,
        norm2_gain,
        norm2_bias,
        weight_up,
        bias_up,
        weight_down,
        bias_down,
    ) = params
    first_low, projected, mixed, log_total, attended, second_low, upward, gelu_low = saved
    down_low = grad_out.astype(jnp.bfloat16)
    grad_bias_down = jnp.sum(grad_out, (0, 1))
    grad_weight_down = jnp.einsum(
        "blf,bld->fd", gelu_low, down_low, preferred_element_type=jnp.float32
    )
    gelu_grad = jnp.einsum("bld,fd->blf", down_low, weight_down, preferred_element_type=jnp.float32)
    gelu_pull = jax.vjp(gelu_smooth, upward)[1]
    up_grad = gelu_pull(gelu_grad)[0]
    grad_bias_up = jnp.sum(up_grad, (0, 1))
    up_low = up_grad.astype(jnp.bfloat16)
    grad_weight_up = jnp.einsum(
        "bld,blf->df", second_low, up_low, preferred_element_type=jnp.float32
    )
    second_grad = jnp.einsum("blf,df->bld", up_low, weight_up, preferred_element_type=jnp.float32)
    second_pull = jax.vjp(layer_norm, attended, norm2_gain, norm2_bias)[1]
    attended_part, grad_norm2_gain, grad_norm2_bias = second_pull(second_grad)
    attended_grad = grad_out + attended_part
    grad_bias_out = jnp.sum(attended_grad, (0, 1))
    attended_low = attended_grad.astype(jnp.bfloat16)
    grad_weight_out = jnp.einsum(
        "bld,ble->de", mixed, attended_low, preferred_element_type=jnp.float32
    )
    mixed_grad = jnp.einsum(
        "ble,de->bld", attended_low, weight_out, preferred_element_type=jnp.float32
    ).astype(jnp.bfloat16)
    projected_grad = attend_backward(projected, segments, log_total, mixed_grad, HEADS)
    grad_weight_qkv = jnp.einsum(
        "bld,ble->de", first_low, projected_grad, preferred_element_type=jnp.float32
    )
    first_grad = jnp.einsum(
        "ble,de->bld", projected_grad, weight_qkv, preferred_element_type=jnp.float32
    )
    first_pull = jax.vjp(layer_norm, hidden, norm1_gain, norm1_bias)[1]
    hidden_part, grad_norm1_gain, grad_norm1_bias = first_pull(first_grad)
    return (
        attended_grad + hidden_part,
        (
            grad_norm1_gain,
            grad_norm1_bias,
            grad_weight_qkv,
            grad_weight_out,
            grad_bias_out,
            grad_norm2_gain,
            grad_norm2_bias,
            grad_weight_up,
            grad_bias_up,
            grad_weight_down,
            grad_bias_down,
        ),
    )


def body(
    inputs,
    cotangent,
    lengths,
    norm1_gain,
    norm1_bias,
    weight_qkv,
    weight_out,
    bias_out,
    norm2_gain,
    norm2_bias,
    weight_up,
    bias_up,
    weight_down,
    bias_down,
):
    params = (
        norm1_gain[0],
        norm1_bias[0],
        weight_qkv[0],
        weight_out[0],
        bias_out[0],
        norm2_gain[0],
        norm2_bias[0],
        weight_up[0],
        bias_up[0],
        weight_down[0],
        bias_down[0],
    )
    section_index = lax.axis_index("section")
    first_section = section_index == 0
    segments = segment_ids(lengths, inputs.shape[2])
    in_text = (segments < lengths.shape[1] - 1).astype(jnp.float32)[..., None]
    rows_micro = inputs.shape[1] // MICRO

    def pick(array, chosen):
        return lax.dynamic_slice_in_dim(array, chosen * rows_micro, rows_micro, 0)

    hidden_list = []
    segment_list = []
    output_list = []
    saved_list = []
    outgoing = None
    for moment in range(MICRO + 1):
        chosen = jnp.clip(moment - section_index, 0, MICRO - 1)
        hidden = pick(inputs[0], chosen).astype(jnp.float32)
        if moment > 0:
            arrived = from_behind(outgoing, "section", 1)
            hidden = hidden + arrived.astype(jnp.float32)
        part_segments = pick(segments, chosen)
        output, saved = layer_forward(params, hidden, part_segments)
        outgoing = output.astype(jnp.bfloat16)
        hidden_list.append(hidden)
        segment_list.append(part_segments)
        output_list.append(outgoing)
        saved_list.append(saved)
    outputs = jnp.concatenate(
        [
            jnp.where(first_section, output_list[index_mb], output_list[index_mb + 1])
            for index_mb in range(MICRO)
        ],
        0,
    )[None]
    zero_grads = tuple((jnp.zeros(param.shape, jnp.float32) for param in params))
    pending = zero_grads
    returned = None
    input_parts = []
    for rewind in range(MICRO + 1):
        moment = MICRO - rewind
        place = moment - section_index
        chosen = jnp.clip(place, 0, MICRO - 1)
        counted = ((place >= 0) & (place <= MICRO - 1)).astype(jnp.float32)
        grad_out = pick(cotangent[0], chosen).astype(jnp.float32) * pick(in_text, chosen)
        if rewind > 0:
            arrived = from_behind(returned, "section", -1)
            grad_out = grad_out + arrived.astype(jnp.float32)
        saved = saved_list[moment]
        hidden_grad, layer_grads = layer_backward(
            params, hidden_list[moment], segment_list[moment], saved, grad_out
        )
        returned = hidden_grad.astype(jnp.bfloat16)
        input_parts.append(hidden_grad)
        pending = tuple((before + counted * fresh for before, fresh in zip(pending, layer_grads)))
    totals = lax.psum(
        (
            pending[0],
            pending[1],
            pending[2],
            pending[3],
            pending[4],
            pending[5],
            pending[6],
            pending[7],
            pending[8],
            pending[9],
            pending[10],
        ),
        "dp",
    )
    input_grad = jnp.concatenate(
        [
            jnp.where(
                first_section, input_parts[MICRO - index_mb], input_parts[MICRO - 1 - index_mb]
            )
            for index_mb in range(MICRO)
        ],
        0,
    )[None]
    return (
        outputs,
        input_grad,
        totals[0][None],
        totals[1][None],
        totals[2][None],
        totals[3][None],
        totals[4][None],
        totals[5][None],
        totals[6][None],
        totals[7][None],
        totals[8][None],
        totals[9][None],
        totals[10][None],
    )


def solution(mesh):
    return jax.shard_map(
        body,
        mesh=mesh,
        in_specs=(
            P("section", "dp", None, None),
            P("section", "dp", None, None),
            P("dp", None),
            P("section", None),
            P("section", None),
            P("section", None, None),
            P("section", None, None),
            P("section", None),
            P("section", None),
            P("section", None),
            P("section", None, None),
            P("section", None),
            P("section", None, None),
            P("section", None),
        ),
        out_specs=(
            P("section", "dp", None, None),
            P("section", "dp", None, None),
            P("section", None),
            P("section", None),
            P("section", None, None),
            P("section", None, None),
            P("section", None),
            P("section", None),
            P("section", None),
            P("section", None, None),
            P("section", None),
            P("section", None, None),
            P("section", None),
        ),
        check_vma=False,
    )
```

profile of v0, /device:TPU:0, one launch (start us, length us, event | category | flops | bytes accessed | tf_op | source)
XLA Modules:
  0.0 937.5 jit_solution(9719400097393285968)
XLA Ops:
  34.6 7.9 fusion.285
  49.9 8.0 fusion
  74.3 5.8 collective-permute-start
  92.4 9.5 %collective-permute-done = bf16[1,1024,512]{1,2,0:T(8,128)(2,1)} collective-permute-done((bf16[1,1024,512]{1,2,0:T(8,128)(2,1)}, bf16[1,1024,512]{1,2,0:T(8,128)(2,1)}, u32[]{:S(2)}, u32[]{:S(2)}) %collective-permute-start) | collective-permute-done | bytes 1048608 | tf_op jit(solution)/shard_map/ppermute | solution.py:18
  121.9 7.9 fusion.288
  137.4 8.0 fusion.2
  157.4 6.7 broadcast_select_fusion.1
  171.3 17.4 %collective-permute-done.1 = bf16[1,1024,512]{1,2,0:T(8,128)(2,1)S(1)} collective-permute-done((bf16[1,1024,512]{1,2,0:T(8,128)(2,1)S(1)}, bf16[1,1024,512]{1,2,0:T(8,128)(2,1)S(1)}, u32[]{:S(2)}, u32[]{:S(2)}) %collective-permute-start.1) | collective-permute-done | bytes 1048608 | tf_op jit(solution)/shard_map/ppermute | solution.py:18
  232.7 8.2 fusion.301
  262.5 8.7 fusion.38
  271.2 10.0 %multiply_reduce_fusion.4 = (f32[8,512]{1,0:T(8,128)}, f32[8,512,1024]{2,1,0:T(8,128)}) fusion(f32[8,512,1024]{2,1,0:T(8,128)S(1)} %bitcast.622, f32[8,512]{1,0:T(8,128)S(1)} %log_add_fusion.4, bf16[1024,8,64]{0,2,1:T(8,128)(2,1)} %bitcast.667, bf16[1,1024,8,64]{1,3,2,0:T(8,128)(2,1)} %bitcast.648), kind=kOutput, calls=%fused_computation.13 | convolution fusion | flops 549449728 | bytes 35160064 | tf_op jit(solution)/shard_map/bqhd,bkhd->bhqk/dot_general | solution.py:96
  281.2 11.6 %multiply_reduce_fusion.5 = (f32[8,512]{1,0:T(8,128)S(1)}, f32[8,512,1024]{2,1,0:T(8,128)}) fusion(f32[8,512,1024]{2,1,0:T(8,128)} %copy-done.6, f32[8,512]{1,0:T(8,128)S(1)} %log_add_fusion.5, bf16[1024,8,64]{0,2,1:T(8,128)(2,1)} %bitcast.668, bf16[1,1024,8,64]{1,3,2,0:T(8,128)(2,1)} %bitcast.649), kind=kOutput, calls=%fused_computation.16 | convolution fusion | flops 549449728 | bytes 35160064 | tf_op jit(solution)/shard_map/bqhd,bkhd->bhqk/dot_general | solution.py:96
  292.8 15.6 %multiply_convert_fusion.5 = bf16[8,512,1024]{2,1,0:T(8,128)(2,1)} fusion(f32[8,512,1024]{2,1,0:T(8,128)} %get-tuple-element.144, f32[8,512,1024]{2,1,0:T(8,128)} %copy-done.6, f32[8,512]{1,0:T(8,128)S(1)} %get-tuple-element.143, f32[8,512]{1,0:T(8,128)S(1)} %log_add_fusion.5), kind=kLoop, calls=%fused_computation.15 | loop fusion | flops 16777216 | bytes 41975808 | tf_op jit(solution)/shard_map/convert_element_type | solution.py:100
  308.4 6.1 fusion.187
  314.6 6.4 fusion.232
  323.3 8.5 add_convert_fusion.2
  331.8 10.2 %multiply_convert_fusion.4 = bf16[8,512,1024]{2,1,0:T(8,128)(2,1)} fusion(f32[8,512,1024]{2,1,0:T(8,128)} %get-tuple-element.146, f32[8,512,1024]{2,1,0:T(8,128)S(1)} %bitcast.622, f32[8,512]{1,0:T(8,128)} %get-tuple-element.145, f32[8,512]{1,0:T(8,128)S(1)} %log_add_fusion.4), kind=kLoop, calls=%fused_computation.12 | loop fusion | flops 16777216 | bytes 41975808 | tf_op jit(solution)/shard_map/convert_element_type | solution.py:100
  342.0 6.5 fusion.186
  366.2 10.7 %fusion.196 = f32[2048,512]{1,0:T(8,128)} fusion(bf16[1,1,1024,512]{2,3,1,0:T(8,128)(2,1)S(1)} %copy-done.79, f32[1024]{0:T(1024)S(1)} %bitcast.733, f32[1024,2048]{1,0:T(8,128)} %copy-done.215, f32[2048]{0:T(1024)S(1)} %bitcast.758), kind=kOutput, calls=%fused_computation.296 | convolution fusion | flops 2170028032 | bytes 13643776 | tf_op jit(solution)/shard_map/blf,bld->fd/dot_general | solution.py:188
  376.9 13.1 %collective-permute-done.2 = bf16[1,1024,512]{1,2,0:T(8,128)(2,1)S(1)} collective-permute-done((bf16[1,1024,512]{1,2,0:T(8,128)(2,1)S(1)}, bf16[1,1024,512]{1,2,0:T(8,128)(2,1)S(1)}, u32[]{:S(2)}, u32[]{:S(2)}) %collective-permute-start.2) | collective-permute-done | bytes 1048608 | tf_op jit(solution)/shard_map/ppermute | solution.py:18
  390.1 8.8 fusion.300
  420.3 8.7 fusion.34
  429.0 10.4 %multiply_reduce_fusion.2 = (f32[8,512]{1,0:T(8,128)}, f32[8,512,1024]{2,1,0:T(8,128)}) fusion(f32[8,512,1024]{2,1,0:T(8,128)S(1)} %bitcast.620, f32[8,512]{1,0:T(8,128)S(1)} %copy-done.129, bf16[1024,8,64]{0,2,1:T(8,128)(2,1)} %bitcast.663, bf16[1,1024,8,64]{1,3,2,0:T(8,128)(2,1)} %bitcast.652), kind=kOutput, calls=%fused_computation.7 | convolution fusion | flops 549449728 | bytes 35160064 | tf_op jit(solution)/shard_map/bqhd,bkhd->bhqk/dot_general | solution.py:96
  439.4 11.5 %multiply_reduce_fusion.3 = (f32[8,512]{1,0:T(8,128)S(1)}, f32[8,512,1024]{2,1,0:T(8,128)}) fusion(f32[8,512,1024]{2,1,0:T(8,128)} %get-tuple-element.132, f32[8,512]{1,0:T(8,128)S(1)} %copy-done.130, bf16[1024,8,64]{0,2,1:T(8,128)(2,1)} %bitcast.664, bf16[1,1024,8,64]{1,3,2,0:T(8,128)(2,1)} %bitcast.653), kind=kOutput, calls=%fused_computation.10 | convolution fusion | flops 549449728 | bytes 35160064 | tf_op jit(solution)/shard_map/bqhd,bkhd->bhqk/dot_general | solution.py:96
  451.0 15.3 %multiply_convert_fusion.3 = bf16[8,512,1024]{2,1,0:T(8,128)(2,1)} fusion(f32[8,512,1024]{2,1,0:T(8,128)} %get-tuple-element.148, f32[8,512,1024]{2,1,0:T(8,128)} %get-tuple-element.132, f32[8,512]{1,0:T(8,128)S(1)} %get-tuple-element.147, f32[8,512]{1,0:T(8,128)S(1)} %copy-done.130), kind=kLoop, calls=%fused_computation.9 | loop fusion | flops 16777216 | bytes 41975808 | tf_op jit(solution)/shard_map/convert_element_type | solution.py:100
  466.3 6.1 fusion.185
  472.4 6.5 fusion.231
  478.9 8.5 add_convert_fusion.1
  487.4 10.3 %multiply_convert_fusion.2 = bf16[8,512,1024]{2,1,0:T(8,128)(2,1)} fusion(f32[8,512,1024]{2,1,0:T(8,128)} %get-tuple-element.150, f32[8,512,1024]{2,1,0:T(8,128)S(1)} %bitcast.620, f32[8,512]{1,0:T(8,128)} %get-tuple-element.149, f32[8,512]{1,0:T(8,128)S(1)} %copy-done.129), kind=kLoop, calls=%fused_computation.6 | loop fusion | flops 16777216 | bytes 41975808 | tf_op jit(solution)/shard_map/convert_element_type | solution.py:100
  497.8 6.5 fusion.184
  534.7 6.6 fusion.242
  541.3 7.1 collective-permute-done.3
  548.4 8.1 fusion.299
  571.8 8.8 fusion.30
  580.6 9.8 %multiply_reduce_fusion = (f32[8,512]{1,0:T(8,128)S(1)}, f32[8,512,1024]{2,1,0:T(8,128)}) fusion(f32[8,512,1024]{2,1,0:T(8,128)S(1)} %bitcast.618, f32[8,512]{1,0:T(8,128)S(1)} %copy-done.127, bf16[1024,8,64]{0,2,1:T(8,128)(2,1)} %bitcast.659, bf16[1,1024,8,64]{1,3,2,0:T(8,128)(2,1)} %bitcast.656), kind=kOutput, calls=%fused_computation.1 | convolution fusion | flops 549449728 | bytes 35160064 | tf_op jit(solution)/shard_map/bqhd,bkhd->bhqk/dot_general | solution.py:96
  590.4 11.6 %multiply_reduce_fusion.1 = (f32[8,512]{1,0:T(8,128)S(1)}, f32[8,512,1024]{2,1,0:T(8,128)}) fusion(f32[8,512,1024]{2,1,0:T(8,128)} %get-tuple-element.126, f32[8,512]{1,0:T(8,128)S(1)} %copy-done.128, bf16[1024,8,64]{0,2,1:T(8,128)(2,1)} %bitcast.660, bf16[1,1024,8,64]{1,3,2,0:T(8,128)(2,1)} %bitcast.657), kind=kOutput, calls=%fused_computation.4 | convolution fusion | flops 549449728 | bytes 35160064 | tf_op jit(solution)/shard_map/bqhd,bkhd->bhqk/dot_general | solution.py:96
  602.0 15.2 %multiply_convert_fusion.1 = bf16[8,512,1024]{2,1,0:T(8,128)(2,1)} fusion(f32[8,512,1024]{2,1,0:T(8,128)} %get-tuple-element.152, f32[8,512,1024]{2,1,0:T(8,128)} %get-tuple-element.126, f32[8,512]{1,0:T(8,128)S(1)} %get-tuple-element.151, f32[8,512]{1,0:T(8,128)S(1)} %copy-done.128), kind=kLoop, calls=%fused_computation.3 | loop fusion | flops 16777216 | bytes 41975808 | tf_op jit(solution)/shard_map/convert_element_type | solution.py:100
  617.2 6.9 fusion.183
  624.1 6.4 fusion.230
  630.5 8.5 add_convert_fusion
  639.1 10.4 %multiply_convert_fusion = bf16[8,512,1024]{2,1,0:T(8,128)(2,1)} fusion(f32[8,512,1024]{2,1,0:T(8,128)} %get-tuple-element.154, f32[8,512,1024]{2,1,0:T(8,128)S(1)} %bitcast.618, f32[8,512]{1,0:T(8,128)S(1)} %get-tuple-element.153, f32[8,512]{1,0:T(8,128)S(1)} %copy-done.127), kind=kLoop, calls=%fused_computation | loop fusion | flops 16777216 | bytes 41975808 | tf_op jit(solution)/shard_map/convert_element_type | solution.py:100
  649.5 6.5 fusion.182
  662.6 8.2 add_bitcast_fusion.1
  677.2 7.0 add_bitcast_fusion
  684.8 8.1 fusion.179
  698.5 5.6 fusion.293
  724.4 61.1 %all-reduce = (f32[1,512]{1,0:T(1,128)}, f32[1,512]{1,0:T(1,128)}, f32[1,512]{1,0:T(1,128)}, f32[1,512]{1,0:T(1,128)}, f32[1,512]{1,0:T(1,128)}, /*index=5*/f32[1,2048]{1,0:T(1,128)}, f32[1,512]{1,0:T(1,128)}) all-reduce(f32[1,512]{1,0:T(1,128)S(1)} %bitcast.754, ...), channel_id=1, replica_groups=mesh['section'=2,'dp'=16] {'dp'}, use_global_device_ids=true, to_apply=%region_47.48 | all-reduce | flops 5120 | bytes 40960 | tf_op jit(solution)/shard_map/psum | solution.py:321
  785.4 134.4 %all-reduce.4.cloned.1.call-done = (f32[1,512,1536]{2,1,0:T(8,128)}, f32[1,512,512]{2,1,0:T(8,128)}, f32[1,512,2048]{2,1,0:T(8,128)}, f32[1,2048,512]{2,1,0:T(8,128)}) async-done(((f32[1,512,1536]{2,1,0:T(8,128)}, f32[1,512,512]{2,1,0:T(8,128)}, f32[1,512,2048]{2,1,0:T(8,128)}, f32[1,2048,512]{2,1,0:T(8,128)}), (f32[1,512,1536]{2,1,0:T(8,128)}, f32[1,512,512]{2,1,0:T(8,128)}, f32[1,512,2048]{2,1,0:T(8,128)}, ...) | async-done | bytes 12582928 | tf_op jit(solution)/shard_map/psum | solution.py:321
  (648 shorter events, 310.4 us)
Async XLA Ops:
  7.2 62.1 %copy-start = (bf16[1,2048,512]{2,1,0:T(8,128)(2,1)S(1)}, bf16[1,2048,512]{2,1,0:T(8,128)(2,1)}, u32[]{:S(2)}) copy-start(bf16[1,2048,512]{2,1,0:T(8,128)(2,1)} %param.26) | copy-start | bytes 6291460
  7.2 912.6 %all-reduce.4.cloned.1.call-start = ((), (), s32[]{:S(2)}) async-start(), calls=%async_computation | async-start | bytes 25165824 | tf_op jit(solution)/shard_map/psum | solution.py:321
  16.7 48.2 %copy-start.14 = (bf16[1,1,1024,512]{2,3,1,0:T(8,128)(2,1)}, bf16[1,1,1024,512]{2,3,1,0:T(8,128)(2,1)S(1)}, u32[]{:S(2)}) copy-start(bf16[1,1,1024,512]{2,3,1,0:T(8,128)(2,1)S(1)} %copy.147) | copy-start | bytes 3145732
  34.6 11.4 %copy-start.1 = (f32[8,512,1024]{2,1,0:T(8,128)}, f32[8,512,1024]{2,1,0:T(8,128)S(1)}, u32[]{:S(2)}) copy-start(f32[8,512,1024]{2,1,0:T(8,128)S(1)} %get-tuple-element.124) | copy-start | bytes 50331652
  49.9 15.0 %copy-start.119 = (bf16[8,64,512]{2,1,0:T(8,128)(2,1)}, bf16[8,64,512]{2,1,0:T(8,128)(2,1)S(1)}, u32[]{:S(2)}) copy-start(bf16[8,64,512]{2,1,0:T(8,128)(2,1)S(1)} %fusion.173) | copy-start | bytes 1572868
  49.9 10.8 %copy-start.2 = (f32[8,512,1024]{2,1,0:T(8,128)S(1)}, f32[8,512,1024]{2,1,0:T(8,128)}, u32[]{:S(2)}) copy-start(f32[8,512,1024]{2,1,0:T(8,128)} %get-tuple-element.126) | copy-start | bytes 50331652
  69.3 10.8 %copy-start.80 = (bf16[1,1,1024,512]{3,2,1,0:T(8,128)(2,1)S(1)}, bf16[1,1,1024,512]{3,2,1,0:T(8,128)(2,1)}, u32[]{:S(2)}) copy-start(bf16[1,1,1024,512]{3,2,1,0:T(8,128)(2,1)} %get-tuple-element.98) | copy-start | bytes 3145732
  74.3 27.6 %collective-permute-start = (bf16[1,1024,512]{1,2,0:T(8,128)(2,1)}, bf16[1,1024,512]{1,2,0:T(8,128)(2,1)}, u32[]{:S(2)}, u32[]{:S(2)}) collective-permute-start(bf16[1,1024,512]{1,2,0:T(8,128)(2,1)} %fusion.157), channel_id=1, source_target_pairs={{0,16},{1,17},{2,18},{3,19},{4,20},{5,21},{6,22},{7,23},{8,24},{9,... | collective-permute-start | bytes 3145736 | tf_op jit(solution)/shard_map/ppermute | solution.py:18
  82.9 69.1 %copy-start.16 = (bf16[1,1,1024,512]{2,3,1,0:T(8,128)(2,1)}, bf16[1,1,1024,512]{2,3,1,0:T(8,128)(2,1)S(1)}, u32[]{:S(2)}) copy-start(bf16[1,1,1024,512]{2,3,1,0:T(8,128)(2,1)S(1)} %copy.148) | copy-start | bytes 3145732
  90.1 15.0 %copy-start.198 = (bf16[1,512,1536]{2,1,0:T(8,128)(2,1)S(1)}, bf16[1,512,1536]{2,1,0:T(8,128)(2,1)}, u32[]{:S(2)}) copy-start(bf16[1,512,1536]{2,1,0:T(8,128)(2,1)} %param.19) | copy-start | bytes 4718596
  121.9 11.4 %copy-start.3 = (f32[8,512,1024]{2,1,0:T(8,128)}, f32[8,512,1024]{2,1,0:T(8,128)S(1)}, u32[]{:S(2)}) copy-start(f32[8,512,1024]{2,1,0:T(8,128)S(1)} %get-tuple-element.130) | copy-start | bytes 50331652
  137.4 14.7 %copy-start.123 = (bf16[8,64,512]{2,1,0:T(8,128)(2,1)}, bf16[8,64,512]{2,1,0:T(8,128)(2,1)S(1)}, u32[]{:S(2)}) copy-start(bf16[8,64,512]{2,1,0:T(8,128)(2,1)S(1)} %fusion.171) | copy-start | bytes 1572868
  137.4 10.8 %copy-start.4 = (f32[8,512,1024]{2,1,0:T(8,128)S(1)}, f32[8,512,1024]{2,1,0:T(8,128)}, u32[]{:S(2)}) copy-start(f32[8,512,1024]{2,1,0:T(8,128)} %get-tuple-element.132) | copy-start | bytes 50331652
  157.3 11.1 %copy-start.176 = (s32[1,1024]{1,0:T(1,128)S(1)}, s32[1,1024]{1,0:T(1,128)}, u32[]{:S(2)}) copy-start(s32[1,1024]{1,0:T(1,128)} %get-tuple-element.114) | copy-start | bytes 12292
  157.3 11.1 %copy-start.183 = (s32[1,512]{1,0:T(1,128)S(1)}, s32[1,512]{1,0:T(1,128)}, u32[]{:S(2)}) copy-start(s32[1,512]{1,0:T(1,128)} %get-tuple-element.108) | copy-start | bytes 6148
  157.3 11.1 %copy-start.184 = (s32[1,512]{1,0:T(1,128)S(1)}, s32[1,512]{1,0:T(1,128)}, u32[]{:S(2)}) copy-start(s32[1,512]{1,0:T(1,128)} %get-tuple-element.109) | copy-start | bytes 6148
  157.3 31.3 %copy-start.36 = (bf16[1,1,1024,512]{2,3,1,0:T(8,128)(2,1)S(1)}, bf16[1,1,1024,512]{2,3,1,0:T(8,128)(2,1)}, u32[]{:S(2)}) copy-start(bf16[1,1,1024,512]{2,3,1,0:T(8,128)(2,1)} %copy.149) | copy-start | bytes 3145732
  164.1 27.6 %copy-start.202 = (bf16[1,1024,512]{1,2,0:T(8,128)(2,1)}, bf16[1,1024,512]{1,2,0:T(8,128)(2,1)S(1)}, u32[]{:S(2)}) copy-start(bf16[1,1024,512]{1,2,0:T(8,128)(2,1)S(1)} %get-tuple-element.142) | copy-start | bytes 3145732
  164.1 25.5 %copy-start.199 = (bf16[1,512,1536]{2,1,0:T(8,128)(2,1)S(1)}, bf16[1,512,1536]{2,1,0:T(8,128)(2,1)}, u32[]{:S(2)}) copy-start(bf16[1,512,1536]{2,1,0:T(8,128)(2,1)} %param.19) | copy-start | bytes 4718596
  164.1 24.6 %collective-permute-start.1 = (bf16[1,1024,512]{1,2,0:T(8,128)(2,1)S(1)}, bf16[1,1024,512]{1,2,0:T(8,128)(2,1)S(1)}, u32[]{:S(2)}, u32[]{:S(2)}) collective-permute-start(bf16[1,1024,512]{1,2,0:T(8,128)(2,1)S(1)} %get-tuple-element.142), channel_id=1, source_target_pairs={{0,16},{1,17},{2,18},{3,19},{4,20},{5,21},{6,22},{7,23},{8,24},{9,... | collective-permute-start | bytes 3145736 | tf_op jit(solution)/shard_map/ppermute | solution.py:18
  167.8 89.9 %copy-start.171 = (f32[1,1024]{1,0:T(1,128)}, f32[1,1024]{1,0:T(1,128)S(1)}, u32[]{:S(2)}) copy-start(f32[1,1024]{1,0:T(1,128)S(1)} %get-tuple-element.106) | copy-start | bytes 12292
  214.9 13.3 %copy-start.115 = (bf16[8,64,512]{2,1,0:T(8,128)(2,1)}, bf16[8,64,512]{2,1,0:T(8,128)(2,1)S(1)}, u32[]{:S(2)}) copy-start(bf16[8,64,512]{2,1,0:T(8,128)(2,1)S(1)} %fusion.169) | copy-start | bytes 1572868
  224.0 68.8 %copy-start.132 = (f32[8,512]{1,0:T(8,128)}, f32[8,512]{1,0:T(8,128)S(1)}, u32[]{:S(2)}) copy-start(f32[8,512]{1,0:T(8,128)S(1)} %log_add_fusion.5) | copy-start | bytes 49156
  229.1 16.0 %copy-start.22 = (f32[1,1024,512]{1,2,0:T(8,128)}, f32[1,1024,512]{1,2,0:T(8,128)S(1)}, u32[]{:S(2)}) copy-start(f32[1,1024,512]{1,2,0:T(8,128)S(1)} %get-tuple-element.140) | copy-start | bytes 6291460
  257.7 13.5 %slice-start.8 = ((s8[16777216]{0:T(1024)(128)(4,1)}), s8[4194304]{0:T(1024)(128)(4,1)S(1)}, s32[]{:S(2)}) async-start(s8[16777216]{0:T(1024)(128)(4,1)} %bitcast.621), calls=%async_computation.9 | async-start | bytes 8388608
  260.7 10.5 %slice-start.9 = ((s8[16777216]{0:T(1024)(128)(4,1)}), s8[4194304]{0:T(1024)(128)(4,1)S(1)}, s32[]{:S(2)}) async-start(s8[16777216]{0:T(1024)(128)(4,1)} %bitcast.621), calls=%async_computation.10 | async-start | bytes 8388608
  292.8 15.6 %copy-start.44 = (bf16[1,1024,512]{1,2,0:T(8,128)(2,1)S(1)}, bf16[1,1024,512]{1,2,0:T(8,128)(2,1)}, u32[]{:S(2)}) copy-start(bf16[1,1024,512]{1,2,0:T(8,128)(2,1)} %copy.125) | copy-start | bytes 3145732
  364.1 26.0 %slice-start.16 = ((s8[8388608]{0:T(1024)(128)(4,1)}), s8[4194304]{0:T(1024)(128)(4,1)S(1)}, s32[]{:S(2)}) async-start(s8[8388608]{0:T(1024)(128)(4,1)} %bitcast.786), calls=%async_computation.17 | async-start | bytes 8388608
  364.6 25.4 %copy-start.87 = (bf16[1,1,1024,512]{2,3,1,0:T(8,128)(2,1)S(1)}, bf16[1,1,1024,512]{2,3,1,0:T(8,128)(2,1)}, u32[]{:S(2)}) copy-start(bf16[1,1,1024,512]{2,3,1,0:T(8,128)(2,1)} %copy.151) | copy-start | bytes 3145732
  364.6 25.4 %copy-start.174 = (f32[1,1024]{1,0:T(1,128)S(1)}, f32[1,1024]{1,0:T(1,128)}, u32[]{:S(2)}) copy-start(f32[1,1024]{1,0:T(1,128)} %get-tuple-element.107) | copy-start | bytes 12292
  364.6 25.4 %slice-start.17 = ((s8[8388608]{0:T(1024)(128)(4,1)}), s8[4194304]{0:T(1024)(128)(4,1)S(1)}, s32[]{:S(2)}) async-start(s8[8388608]{0:T(1024)(128)(4,1)} %bitcast.786), calls=%async_computation.18 | async-start | bytes 8388608
  364.6 25.4 %collective-permute-start.2 = (bf16[1,1024,512]{1,2,0:T(8,128)(2,1)S(1)}, bf16[1,1024,512]{1,2,0:T(8,128)(2,1)S(1)}, u32[]{:S(2)}, u32[]{:S(2)}) collective-permute-start(bf16[1,1024,512]{1,2,0:T(8,128)(2,1)S(1)} %fusion.217), channel_id=1, source_target_pairs={{16,0},{17,1},{18,2},{19,3},{20,4},{21,5},{22,6},{23,7},{24,8},{25... | collective-permute-start | bytes 3145736 | tf_op jit(solution)/shard_map/ppermute | solution.py:18
  415.5 13.6 %slice-start.4 = ((s8[16777216]{0:T(1024)(128)(4,1)}), s8[4194304]{0:T(1024)(128)(4,1)S(1)}, s32[]{:S(2)}) async-start(s8[16777216]{0:T(1024)(128)(4,1)} %bitcast.619), calls=%async_computation.5 | async-start | bytes 8388608
  415.5 13.6 %slice-start.5 = ((s8[16777216]{0:T(1024)(128)(4,1)}), s8[4194304]{0:T(1024)(128)(4,1)S(1)}, s32[]{:S(2)}) async-start(s8[16777216]{0:T(1024)(128)(4,1)} %bitcast.619), calls=%async_computation.6 | async-start | bytes 8388608
  429.0 10.4 %copy-start.130 = (f32[8,512]{1,0:T(8,128)S(1)}, f32[8,512]{1,0:T(8,128)}, u32[]{:S(2)}) copy-start(f32[8,512]{1,0:T(8,128)} %log_add_fusion.3) | copy-start | bytes 49156
  451.0 15.3 %copy-start.42 = (bf16[1,1024,512]{1,2,0:T(8,128)(2,1)S(1)}, bf16[1,1024,512]{1,2,0:T(8,128)(2,1)}, u32[]{:S(2)}) copy-start(bf16[1,1024,512]{1,2,0:T(8,128)(2,1)} %copy.120) | copy-start | bytes 3145732
  524.0 24.3 %collective-permute-start.3 = (bf16[1,1024,512]{1,2,0:T(8,128)(2,1)S(1)}, bf16[1,1024,512]{1,2,0:T(8,128)(2,1)S(1)}, u32[]{:S(2)}, u32[]{:S(2)}) collective-permute-start(bf16[1,1024,512]{1,2,0:T(8,128)(2,1)S(1)} %get-tuple-element.81), channel_id=1, source_target_pairs={{16,0},{17,1},{18,2},{19,3},{20,4},{21,5},{22,6},{23,7},{24,8},{25... | collective-permute-start | bytes 3145736 | tf_op jit(solution)/shard_map/ppermute | solution.py:18
  531.0 17.4 %slice-start.12 = ((s8[8388608]{0:T(1024)(128)(4,1)}), s8[4194304]{0:T(1024)(128)(4,1)S(1)}, s32[]{:S(2)}) async-start(s8[8388608]{0:T(1024)(128)(4,1)} %bitcast.782), calls=%async_computation.13 | async-start | bytes 8388608
  534.7 13.7 %copy-start.85 = (bf16[1,1,1024,512]{2,3,1,0:T(8,128)(2,1)S(1)}, bf16[1,1,1024,512]{2,3,1,0:T(8,128)(2,1)}, u32[]{:S(2)}) copy-start(bf16[1,1,1024,512]{2,3,1,0:T(8,128)(2,1)} %copy.150) | copy-start | bytes 3145732
  534.7 13.7 %copy-start.173 = (f32[1,1024]{1,0:T(1,128)S(1)}, f32[1,1024]{1,0:T(1,128)}, u32[]{:S(2)}) copy-start(f32[1,1024]{1,0:T(1,128)} %get-tuple-element.105) | copy-start | bytes 12292
  534.7 13.7 %slice-start.13 = ((s8[8388608]{0:T(1024)(128)(4,1)}), s8[4194304]{0:T(1024)(128)(4,1)S(1)}, s32[]{:S(2)}) async-start(s8[8388608]{0:T(1024)(128)(4,1)} %bitcast.782), calls=%async_computation.14 | async-start | bytes 8388608
  567.6 13.0 %slice-start = ((s8[16777216]{0:T(1024)(128)(4,1)}), s8[4194304]{0:T(1024)(128)(4,1)S(1)}, s32[]{:S(2)}) async-start(s8[16777216]{0:T(1024)(128)(4,1)} %bitcast.617), calls=%async_computation.1 | async-start | bytes 8388608
  567.6 13.0 %slice-start.1 = ((s8[16777216]{0:T(1024)(128)(4,1)}), s8[4194304]{0:T(1024)(128)(4,1)S(1)}, s32[]{:S(2)}) async-start(s8[16777216]{0:T(1024)(128)(4,1)} %bitcast.617), calls=%async_computation.2 | async-start | bytes 8388608
  580.6 9.8 %copy-start.128 = (f32[8,512]{1,0:T(8,128)S(1)}, f32[8,512]{1,0:T(8,128)}, u32[]{:S(2)}) copy-start(f32[8,512]{1,0:T(8,128)} %log_add_fusion.1) | copy-start | bytes 49156
  602.0 15.2 %copy-start.40 = (bf16[1,1024,512]{1,2,0:T(8,128)(2,1)S(1)}, bf16[1,1024,512]{1,2,0:T(8,128)(2,1)}, u32[]{:S(2)}) copy-start(bf16[1,1024,512]{1,2,0:T(8,128)(2,1)} %copy.115) | copy-start | bytes 3145732
  656.1 19.6 %slice-start.14 = ((s8[8388608]{0:T(1024)(128)(4,1)}), s8[4194304]{0:T(1024)(128)(4,1)S(1)}, s32[]{:S(2)}) async-start(s8[8388608]{0:T(1024)(128)(4,1)} %bitcast.784), calls=%async_computation.15 | async-start | bytes 8388608
  659.5 11.5 %copy-start.91 = (bf16[8,64,1024]{2,1,0:T(8,128)(2,1)}, bf16[8,64,1024]{2,1,0:T(8,128)(2,1)S(1)}, u32[]{:S(2)}) copy-start(bf16[8,64,1024]{2,1,0:T(8,128)(2,1)S(1)} %multiply_convert_fusion.9) | copy-start | bytes 3145732
  662.6 13.1 %slice-start.15 = ((s8[8388608]{0:T(1024)(128)(4,1)}), s8[4194304]{0:T(1024)(128)(4,1)S(1)}, s32[]{:S(2)}) async-start(s8[8388608]{0:T(1024)(128)(4,1)} %bitcast.784), calls=%async_computation.16 | async-start | bytes 8388608
  (199 other events, 851.5 us)
Sparse Core Ops, SparseCore 0:
  684.3 235.4 all-reduce.3
where the time goes:
time: 947 us; the launch traced here: 938 us
  matrix products  392 us (41%)
  waiting for transfers between devices  181 us (19%)
  other arithmetic  164 us (17%)
  local copies, waits for them, and re-layouts  110 us (12%)
  blocking collectives  61.1 us (6%)
  between operations  17.3 us (2%)
  starting transfers between devices  12.1 us (1%)
    psum x1, waiting for transfers between devices, body(): lax.psum((pending[0], pending[1], pending[2], pending[3], pending[4], pen...  134 us
    convert_element_type x6, other arithmetic, attend_backward(): score_grad = (probs * (prob_grad - inner)).astype(jnp.bfloat16)  77 us
    dot_general x6, matrix products, attend_backward(): jnp.einsum('bqhd,bkhd->bhqk', block_out, values_all, preferred_element_ty...  64.8 us
    psum x1, blocking collectives, body(): lax.psum((pending[0], pending[1], pending[2], pending[3], pending[4], pen...  61.1 us
    unnamed x496, local copies, waits for them, and re-layouts  58.6 us
    dot_general x6, matrix products, attend_backward(): jnp.einsum('bhqk,bqhd->bkhd', probs.astype(jnp.bfloat16), block_out, pref...  51.8 us
    ppermute x4, waiting for transfers between devices, from_behind(): return lax.ppermute(block, axis, route)  47 us
    dot_general x6, matrix products, attend_backward(): jnp.einsum('bhqk,bkhd->bqhd', score_grad, keys_all, preferred_element_typ...  38.7 us
  transfers between devices with their start and end apart: 5, of which 5 were waited for; matrix products, arithmetic and copies ran while one was open for 9% of the time, Pallas kernels for 0%

commit v1 on v0

v1 whole, which is shorter than its diff:
```python
import functools

import jax
import jax.numpy as jnp
from jax import lax
from jax.experimental import pallas as pl
from jax.experimental.pallas import tpu as pltpu
from jax.sharding import PartitionSpec as P

EPSILON = 1e-05
GELU_C = 0.7978845608028654
MASKED = -1e30
TILE = 256
CHUNK = 512
BF = jnp.bfloat16
F32 = jnp.float32
MESH = pl.DeviceIdType.MESH
ANY = pl.BlockSpec(memory_space=pl.ANY)
VMEM = pl.BlockSpec(memory_space=pltpu.VMEM)
SMEM = pl.BlockSpec(memory_space=pltpu.SMEM)


def dot(a, b):
    return jnp.dot(a, b, preferred_element_type=F32)


def dot_nt(a, b):
    return lax.dot_general(a, b, (((1,), (1,)), ((), ())), preferred_element_type=F32)


def dot_tn(a, b):
    return lax.dot_general(a, b, (((0,), (0,)), ((), ())), preferred_element_type=F32)


def norm_parts(v):
    centred = v - jnp.mean(v, -1, keepdims=True)
    rstd = lax.rsqrt(jnp.mean(centred * centred, -1, keepdims=True) + EPSILON)
    return centred * rstd, rstd


def norm_pull(grad, hat, rstd, gain):
    scaled = grad * gain
    return rstd * (
        scaled
        - jnp.mean(scaled, -1, keepdims=True)
        - hat * jnp.mean(scaled * hat, -1, keepdims=True)
    )


def colsum(v):
    return jnp.sum(v, 0, keepdims=True)


def stack_pair(block):
    lane = lax.broadcasted_iota(jnp.int32, block.shape, 1)
    zero = jnp.zeros_like(block)
    low = lane < 64
    return jnp.concatenate([jnp.where(low, block, zero), jnp.where(low, zero, block)], 0)


def unstack_pair(both):
    rows = both.shape[0] // 2
    lane = lax.broadcasted_iota(jnp.int32, (rows, 128), 1)
    return jnp.where(lane < 64, both[:rows], both[rows:])


def tile_rows(t):
    return pl.ds(pl.multiple_of(t * TILE, TILE), TILE)


def for_spans(lengths, row, length, run):
    def body(s, first):
        last = first + lengths[row, s]
        base = (first // 16) * 16
        need = last - base

        def case(above, window):
            @pl.when((need > above) & (need <= window))
            def _():
                start = pl.multiple_of(jnp.minimum(base, length - window), 16)
                run(start, first, last, window)

        case(0, 128)
        case(128, 256)
        case(256, 384)
        return last

    lax.fori_loop(0, lengths.shape[1], body, 0)


def pick(pair):
    return pair[0] + lax.axis_index("section") * (pair[1] - pair[0])


def forward_kernel(rows_of, *refs):
    n_alias = len(refs) - 15 - 6 - 13
    (lengths, x_any, arr_any, wqkv_any, wo_any, wu_any, wd_any, n1g, n1b, bo, n2g, n2b, bu, bd) = refs[:14]
    (out_any, proj_any, mixed_any, att_any, up_any, snd_any,
     x, arr, wqkv, wo, wu, wd, proj, mixed, out, att, up, sem_in, sem_out) = refs[len(refs) - 19:]
    row = pick(rows_of)
    T, D = x.shape
    FF = up.shape[1]
    n_tiles = T // TILE
    second_section = lax.axis_index("section") == 1

    @pl.when(row >= 0)
    def _():
        copies = [
            pltpu.make_async_copy(s, d, sem_in.at[k])
            for k, (s, d) in enumerate(
                [(x_any.at[row], x), (wqkv_any, wqkv), (wo_any, wo), (wu_any, wu), (wd_any, wd), (arr_any, arr)]
            )
        ]

        @pl.when(second_section)
        def _():
            copies[5].start()

        for c in copies[:5]:
            c.start()

        @pl.when(second_section)
        def _():
            copies[5].wait()

        @pl.when(jnp.logical_not(second_section))
        def _():
            arr[...] = jnp.zeros_like(arr)

        copies[0].wait()
        copies[1].wait()

        def sends(t, group, pairs):
            rows = tile_rows(t)
            return [pltpu.make_async_copy(s.at[rows], d.at[rows], sem_out.at[group + k, t])
                    for k, (s, d) in enumerate(pairs)]

        pairs_a = [(proj, proj_any.at[row])]
        pairs_b = [(out, out_any.at[row]), (out, snd_any), (att, att_any.at[row]), (up, up_any.at[row])]

        def qkv_tile(t, carry):
            rows = tile_rows(t)
            h = x[rows, :].astype(F32) + arr[rows, :].astype(F32)
            first = (norm_parts(h)[0] * n1g[...] + n1b[...]).astype(BF)
            for c in range(0, 3 * D, CHUNK):
                proj[rows, c:c + CHUNK] = dot(first, wqkv[:, c:c + CHUNK]).astype(BF)
            for c in sends(t, 0, pairs_a):
                c.start()
            return carry

        lax.fori_loop(0, n_tiles, qkv_tile, 0)

        def run(start, first, last, window):
            rows = pl.ds(start, window)
            pos = start + lax.broadcasted_iota(jnp.int32, (1, window), 1)
            kmask = jnp.where((pos >= first) & (pos < last), 0.0, MASKED)
            qpos = start + lax.broadcasted_iota(jnp.int32, (window, 128), 0)
            keep = (qpos >= first) & (qpos < last)
            ones = jnp.ones((window, 128), BF)
            for p in range(D // 128):
                cq = slice(p * 128, p * 128 + 128)
                q = stack_pair(proj[rows, cq] * jnp.asarray(0.125, BF))
                k = proj[rows, D + p * 128:D + p * 128 + 128]
                v = proj[rows, 2 * D + p * 128:2 * D + p * 128 + 128]
                s = dot_nt(q, k) + kmask
                e = jnp.exp(s - jnp.max(s, -1, keepdims=True)).astype(BF)
                o = dot(e, jnp.concatenate([v, ones], 1))
                o = unstack_pair(o[:, :128] / o[:, 128:])
                mixed[rows, cq] = jnp.where(keep, o.astype(BF), mixed[rows, cq])

        for_spans(lengths, row, T, run)
        mixed_out = pltpu.make_async_copy(mixed, mixed_any.at[row], sem_out.at[5, 0])
        mixed_out.start()
        for c in copies[2:5]:
            c.wait()

        def post_tile(t, carry):
            rows = tile_rows(t)
            h = x[rows, :].astype(F32) + arr[rows, :].astype(F32)
            a = h + dot(mixed[rows, :], wo[...]) + bo[...]
            att[rows, :] = a
            second = (norm_parts(a)[0] * n2g[...] + n2b[...]).astype(BF)
            total = a + bd[...]
            for c in range(0, FF, CHUNK):
                u = dot(second, wu[:, c:c + CHUNK]) + bu[:, c:c + CHUNK]
                up[rows, c:c + CHUNK] = u.astype(BF)
                total = total + dot(jax.nn.gelu(u, approximate=True).astype(BF), wd[c:c + CHUNK, :])
            out[rows, :] = total.astype(BF)
            for c in sends(t, 1, pairs_b):
                c.start()
            return carry

        lax.fori_loop(0, n_tiles, post_tile, 0)
        mixed_out.wait()
        for t in range(n_tiles):
            for c in sends(t, 0, pairs_a) + sends(t, 1, pairs_b):
                c.wait()


def forward(rows_of, lengths, x, arr, w, saved):
    n, T, D = x.shape
    FF = w["wu"].shape[1]
    S, V = jax.ShapeDtypeStruct, pltpu.VMEM
    outs = [S((n, T, D), BF), S((n, T, 3 * D), BF), S((n, T, D), BF), S((n, T, D), F32), S((n, T, FF), BF), S((T, D), BF)]
    return pl.pallas_call(
        functools.partial(forward_kernel, rows_of),
        out_shape=outs,
        in_specs=[SMEM] + [ANY] * 6 + [VMEM] * 7 + [ANY] * len(saved),
        out_specs=[ANY] * 6,
        input_output_aliases={14 + i: i for i in range(len(saved))},
        scratch_shapes=[
            V((T, D), BF), V((T, D), BF), V((D, 3 * D), BF), V((D, D), BF), V((D, FF), BF), V((FF, D), BF),
            V((T, 3 * D), BF), V((T, D), BF), V((T, D), BF), V((T, D), F32), V((T, FF), BF),
            pltpu.SemaphoreType.DMA((6,)), pltpu.SemaphoreType.DMA((6, T // TILE)),
        ],
        compiler_params=pltpu.CompilerParams(vmem_limit_bytes=48 * 2**20),
        cost_estimate=pl.CostEstimate(flops=8 * 10**9, bytes_accessed=20 * 2**20, transcendentals=0),
        name="row_forward",
    )(lengths, x, arr, w["wqkv"], w["wo"], w["wu"], w["wd"], w["n1g"], w["n1b"], w["bo"], w["n2g"], w["n2b"],
      w["bu"], w["bd"], *saved)


def backward_kernel(rows_of, *refs):
    (lengths, x_any, arr_any, cot_any, ret_any, proj_any, att_any, up_any,
     wqkv_any, wo_any, wu_any, wd_any, n1g, n1b, n2g, n2b) = refs[:16]
    (dh_any, first_any, dproj_any, al_any, second_any, ul_any, gelu_any, gl_any, snd_any, vec_out,
     x, arr, cot, ret, proj, att, up, wqkv, wo, wu, wd,
     dproj, dmix, da, first, al, second, ul, gl, dh, snd, sem_in, sem_out) = refs[len(refs) - 33:]
    row = pick(rows_of)
    T, D = x.shape
    FF = up.shape[1]
    n_tiles = T // TILE
    second_section = lax.axis_index("section") == 1
    vec_out[...] = jnp.zeros_like(vec_out)

    @pl.when(row >= 0)
    def _():
        def load(k, source, target):
            return pltpu.make_async_copy(source, target, sem_in.at[k])

        def load_up(t):
            return load(t, up_any.at[row, tile_rows(t)], up.at[tile_rows(t)])

        k0 = n_tiles
        c_cot = load(k0, cot_any.at[row], cot)
        c_wd = load(k0 + 1, wd_any, wd)
        c_wu = load(k0 + 2, wu_any, wu)
        c_att = load(k0 + 3, att_any.at[row], att)
        c_wo = load(k0 + 4, wo_any, wo)
        c_proj = load(k0 + 5, proj_any.at[row], proj)
        c_x = load(k0 + 6, x_any.at[row], x)
        c_wqkv = load(k0 + 7, wqkv_any, wqkv)
        c_arr = load(k0 + 8, arr_any, arr)
        c_ret = load(k0 + 9, ret_any, ret)

        @pl.when(jnp.logical_not(second_section))
        def _():
            c_ret.start()

        for c in [c_cot, c_wd, load_up(0), c_wu, c_att, c_wo] + [load_up(t) for t in range(1, n_tiles)]:
            c.start()
        for c in [c_proj, c_wqkv, c_x]:
            c.start()

        @pl.when(second_section)
        def _():
            c_arr.start()
            ret[...] = jnp.zeros_like(ret)

        @pl.when(jnp.logical_not(second_section))
        def _():
            arr[...] = jnp.zeros_like(arr)
            c_ret.wait()

        for c in (c_cot, c_wd, c_wu, c_att, c_wo):
            c.wait()

        def sends(t, group, pairs):
            rows = tile_rows(t)
            return [pltpu.make_async_copy(s.at[rows], d.at[rows], sem_out.at[group + k, t])
                    for k, (s, d) in enumerate(pairs)]

        pairs_a = [(s, d.at[row]) for s, d in
                   [(gl, gl_any), (up, gelu_any), (ul, ul_any), (second, second_any), (al, al_any)]]
        pairs_b = [(first, first_any.at[row]), (dproj, dproj_any.at[row]), (dh, dh_any.at[row]), (snd, snd_any)]
        text_end = T - lengths[row, lengths.shape[1] - 1]

        def pre_tile(t, carry):
            rows = tile_rows(t)
            load_up(t).wait()
            pos = t * TILE + lax.broadcasted_iota(jnp.int32, (TILE, 1), 0)
            in_text = (pos < text_end).astype(F32)
            g = cot[rows, :].astype(F32) * in_text + ret[rows, :].astype(F32)
            g_low = g.astype(BF)
            gl[rows, :] = g_low
            vec_out[5:6, :] += colsum(g)
            sg = jnp.zeros((TILE, D), F32)
            for c in range(0, FF, CHUNK):
                cc = slice(c, c + CHUNK)
                u = up[rows, cc].astype(F32)
                uu = u * u
                th = jnp.tanh(u * (GELU_C + (GELU_C * 0.044715) * uu))
                half = 0.5 * (1.0 + th)
                up[rows, cc] = (u * half).astype(BF)
                slope = half + (0.5 * u) * (1.0 - th * th) * (GELU_C + (3.0 * GELU_C * 0.044715) * uu)
                ug = dot_nt(g_low, wd[cc, :]) * slope
                vec_out[6 + c // CHUNK:7 + c // CHUNK, :] += colsum(ug)
                ug_low = ug.astype(BF)
                ul[rows, cc] = ug_low
                sg = sg + dot_nt(ug_low, wu[:, cc])
            hat, rstd = norm_parts(att[rows, :])
            second[rows, :] = (hat * n2g[...] + n2b[...]).astype(BF)
            vec_out[3:4, :] += colsum(sg * hat)
            vec_out[4:5, :] += colsum(sg)
            a = g + norm_pull(sg, hat, rstd, n2g[...])
            vec_out[2:3, :] += colsum(a)
            da[rows, :] = a
            a_low = a.astype(BF)
            al[rows, :] = a_low
            dmix[rows, :] = dot_nt(a_low, wo[...]).astype(BF)
            for c in sends(t, 0, pairs_a):
                c.start()
            return carry

        lax.fori_loop(0, n_tiles, pre_tile, 0)
        c_proj.wait()

        def run(start, first_pos, last_pos, window):
            rows = pl.ds(start, window)
            pos = start + lax.broadcasted_iota(jnp.int32, (window, 128), 0)
            keep = (pos >= first_pos) & (pos < last_pos)
            kcol = start + lax.broadcasted_iota(jnp.int32, (window, 1), 0)
            kmask = jnp.where((kcol >= first_pos) & (kcol < last_pos), 0.0, MASKED)
            zero = jnp.zeros((window, 128), BF)
            eighth = jnp.asarray(0.125, BF)
            for p in range(D // 128):
                cq = slice(p * 128, p * 128 + 128)
                ck = slice(D + p * 128, D + p * 128 + 128)
                cv = slice(2 * D + p * 128, 2 * D + p * 128 + 128)
                q = stack_pair(proj[rows, cq] * eighth)
                k = proj[rows, ck]
                v = proj[rows, cv]
                do = stack_pair(jnp.where(keep, dmix[rows, cq], zero))
                s = dot_nt(k, q) + kmask
                e = jnp.exp(s - jnp.max(s, 0, keepdims=True))
                prob = e * (1.0 / jnp.sum(e, 0, keepdims=True))
                dp = dot_nt(v, do)
                inner = jnp.sum(dp * prob, 0, keepdims=True)
                ds = (prob * (dp - inner)).astype(BF)
                dv = dot(prob.astype(BF), do)
                dk = dot(ds, q)
                dq = unstack_pair(dot_tn(ds, k * eighth))
                dproj[rows, cq] = jnp.where(keep, dq.astype(BF), dproj[rows, cq])
                dproj[rows, ck] = jnp.where(keep, dk.astype(BF), dproj[rows, ck])
                dproj[rows, cv] = jnp.where(keep, dv.astype(BF), dproj[rows, cv])

        for_spans(lengths, row, T, run)
        c_wqkv.wait()
        c_x.wait()

        @pl.when(second_section)
        def _():
            c_arr.wait()

        def fin_tile(t, carry):
            rows = tile_rows(t)
            fg = dot_nt(dproj[rows, :], wqkv[...])
            hat, rstd = norm_parts(x[rows, :].astype(F32) + arr[rows, :].astype(F32))
            first[rows, :] = (hat * n1g[...] + n1b[...]).astype(BF)
            vec_out[0:1, :] += colsum(fg * hat)
            vec_out[1:2, :] += colsum(fg)
            d = da[rows, :] + norm_pull(fg, hat, rstd, n1g[...])
            dh[rows, :] = d
            snd[rows, :] = d.astype(BF)
            for c in sends(t, 5, pairs_b):
                c.start()
            return carry

        lax.fori_loop(0, n_tiles, fin_tile, 0)
        for t in range(n_tiles):
            for c in sends(t, 0, pairs_a) + sends(t, 5, pairs_b):
                c.wait()


def backward(rows_of, lengths, x, arr, cot, ret, saved, w, kept):
    proj, mixed, att, up = saved
    n, T, D = x.shape
    FF = up.shape[2]
    S, V = jax.ShapeDtypeStruct, pltpu.VMEM
    outs = [
        S((n, T, D), F32), S((n, T, D), BF), S((n, T, 3 * D), BF), S((n, T, D), BF), S((n, T, D), BF),
        S((n, T, FF), BF), S((n, T, FF), BF), S((n, T, D), BF), S((T, D), BF), S((16, CHUNK), F32),
    ]
    return pl.pallas_call(
        functools.partial(backward_kernel, rows_of),
        out_shape=outs,
        in_specs=[SMEM] + [ANY] * 11 + [VMEM] * 4 + [ANY] * len(kept),
        out_specs=[ANY] * 9 + [VMEM],
        input_output_aliases={16 + i: i for i in range(len(kept))},
        scratch_shapes=[
            V((T, D), BF), V((T, D), BF), V((T, D), BF), V((T, D), BF), V((T, 3 * D), BF), V((T, D), F32), V((T, FF), BF),
            V((D, 3 * D), BF), V((D, D), BF), V((D, FF), BF), V((FF, D), BF),
            V((T, 3 * D), BF), V((T, D), BF), V((T, D), F32), V((T, D), BF), V((T, D), BF), V((T, D), BF), V((T, FF), BF),
            V((T, D), BF), V((T, D), F32), V((T, D), BF),
            pltpu.SemaphoreType.DMA((10 + T // TILE,)), pltpu.SemaphoreType.DMA((9, T // TILE)),
        ],
        compiler_params=pltpu.CompilerParams(vmem_limit_bytes=56 * 2**20),
        cost_estimate=pl.CostEstimate(flops=14 * 10**9, bytes_accessed=37 * 2**20, transcendentals=0),
        name="row_backward",
    )(lengths, x, arr, cot, ret, proj, att, up, w["wqkv"], w["wo"], w["wu"], w["wd"], w["n1g"], w["n1b"], w["n2g"],
      w["n2b"], *kept)


def reduce_kernel(n, *refs):
    bits = n.bit_length() - 1
    (gelu_any, gl_any, second_any, ul_any, mixed_any, al_any, first_any, dproj_any, vec_a, vec_b, vec_c) = refs[:11]
    (wd_out, wu_out, wo_out, wqkv_out, vec_out) = refs[11:16]
    left, right, total, final, *rest = refs[16:]
    inbox = rest[:bits]
    (vec_box, stage, vec_tmp, sem_load, sem_store, rs_send, rs_recv, ag_send, ag_recv, vec_send, vec_recv) = rest[bits:]
    n_chunks = total.shape[0]
    FF = gelu_any.shape[2]
    D = gl_any.shape[2]
    T = gl_any.shape[1]
    rows = gl_any.shape[0]
    ff_chunks = FF // CHUNK
    me = lax.axis_index("dp")
    value = [(me // 2**b) % 2 for b in range(bits)]
    partner = [me + (1 - 2 * value[b]) * 2**b for b in range(bits)]
    size = total.shape[1]

    barrier = pltpu.get_barrier_semaphore()
    for b in range(bits):
        pl.semaphore_signal(barrier, inc=1, device_id={"dp": partner[b]}, device_id_type=MESH)
    pl.semaphore_wait(barrier, bits)

    base = [0]
    for b in range(bits):
        base.append(base[-1] + value[b] * (size >> (b + 1)))

    def halve(c, b):
        half = size >> (b + 1)
        away = pl.multiple_of(base[b] + (1 - value[b]) * half, half)
        return pltpu.make_async_remote_copy(
            src_ref=total.at[c, pl.ds(away, half)], dst_ref=inbox[b].at[c],
            send_sem=rs_send.at[c, b], recv_sem=rs_recv.at[c, b],
            device_id={"dp": partner[b]}, device_id_type=MESH,
        )

    def double(c, b):
        half = size >> (b + 1)
        here = final.at[c, pl.ds(pl.multiple_of(base[b + 1], half), half)]
        return pltpu.make_async_remote_copy(
            src_ref=here, dst_ref=here,
            send_sem=ag_send.at[c, b], recv_sem=ag_recv.at[c, b],
            device_id={"dp": partner[b]}, device_id_type=MESH,
        )

    def add_in(c, b):
        half = size >> (b + 1)
        mine = pl.ds(pl.multiple_of(base[b + 1], half), half)
        target = total if b + 1 < bits else final
        target[c, mine, :] = (total[c, mine, :].astype(F32) + inbox[b][c].astype(F32)).astype(BF)

    def load(c, slot, act):
        def both(a, b):
            for k, (source, target) in enumerate(((a, left), (b, right))):
                act(pltpu.make_async_copy(source, target.at[slot], sem_load.at[k, slot]))

        def cols(ref, j):
            return ref.at[:, :, pl.ds(pl.multiple_of(j * CHUNK, CHUNK), CHUNK)]

        @pl.when(c < ff_chunks)
        def _():
            both(cols(gelu_any, c), gl_any)

        @pl.when((c >= ff_chunks) & (c < 2 * ff_chunks))
        def _():
            both(second_any, cols(ul_any, c - ff_chunks))

        @pl.when(c == 2 * ff_chunks)
        def _():
            both(mixed_any, al_any)

        @pl.when((c > 2 * ff_chunks) & (c < n_chunks))
        def _():
            both(first_any, cols(dproj_any, c - 2 * ff_chunks - 1))

    def store(c, slot, act):
        def block(target):
            act(pltpu.make_async_copy(stage.at[slot], target, sem_store.at[slot]))

        def cols(ref, j):
            return ref.at[:, pl.ds(pl.multiple_of(j * CHUNK, CHUNK), CHUNK)]

        @pl.when((c >= 0) & (c < ff_chunks))
        def _():
            block(wd_out.at[pl.ds(pl.multiple_of(c * CHUNK, CHUNK), CHUNK)])

        @pl.when((c >= ff_chunks) & (c < 2 * ff_chunks))
        def _():
            block(cols(wu_out, c - ff_chunks))

        @pl.when(c == 2 * ff_chunks)
        def _():
            block(wo_out)

        @pl.when(c > 2 * ff_chunks)
        def _():
            block(cols(wqkv_out, c - 2 * ff_chunks - 1))

    def vec_copy(b):
        return pltpu.make_async_remote_copy(
            src_ref=vec_tmp.at[b], dst_ref=vec_box.at[b],
            send_sem=vec_send.at[b], recv_sem=vec_recv.at[b],
            device_id={"dp": partner[b]}, device_id_type=MESH,
        )

    vec_tmp[0] = vec_a[...] + vec_b[...] + vec_c[...]
    vec_copy(0).start()
    load(jnp.int32(0), 0, lambda c: c.start())

    def slot_step(t, carry):
        def stage_of(lag, act):
            c = t - lag

            @pl.when((c >= 0) & (c < n_chunks))
            def _():
                act(c)

        def make(c):
            slot = lax.rem(c, 2)
            load(c + 1, 1 - slot, lambda d: d.start())
            load(c, slot, lambda d: d.wait())
            a = left[slot].reshape(rows * T, CHUNK)
            b = right[slot].reshape(rows * T, CHUNK)
            g = dot_tn(a, b).astype(BF)
            total[c, :CHUNK, :] = g[:, :CHUNK // 2]
            total[c, CHUNK:, :] = g[:, CHUNK // 2:]
            halve(c, 0).start()

        def reduce_step(b):
            def act(c):
                halve(c, b).wait()
                add_in(c, b)
                if b + 1 < bits:
                    halve(c, b + 1).start()
                else:
                    double(c, b).start()
            return act

        def gather_step(b):
            def act(c):
                double(c, b).wait()
                double(c, b - 1).start()
            return act

        def finish(c):
            slot = lax.rem(c, 2)
            double(c, 0).wait()

            @pl.when(c >= 2)
            def _():
                store(c - 2, slot, lambda d: d.wait())

            stage[slot, :, :CHUNK // 2] = final[c, :CHUNK, :]
            stage[slot, :, CHUNK // 2:] = final[c, CHUNK:, :]
            store(c, slot, lambda d: d.start())

        stage_of(0, make)
        stage_of(1, reduce_step(0))
        for b in range(bits - 1, 0, -1):
            stage_of(bits + (bits - b), gather_step(b))
        for b in range(1, bits):
            stage_of(1 + b, reduce_step(b))
        stage_of(2 * bits, finish)
        return carry

    lax.fori_loop(0, n_chunks + 2 * bits, slot_step, 0)
    for b in range(bits):
        vec_copy(b).wait()
        merged = vec_tmp[b] + vec_box[b]
        if b + 1 < bits:
            vec_tmp[b + 1] = merged
            vec_copy(b + 1).start()
        else:
            vec_out[...] = merged
    for c in (n_chunks - 2, n_chunks - 1):
        store(jnp.int32(c), c % 2, lambda d: d.wait())


def weight_grads(n, mixed, kept, vecs):
    dh, first, dproj, al, second, ul, gelu, gl = kept
    rows, T, D = gl.shape
    FF = ul.shape[2]
    bits = n.bit_length() - 1
    n_chunks = 2 * (FF // CHUNK) + 1 + 3 * D // CHUNK
    size = CHUNK * 2
    S, V, DMA = jax.ShapeDtypeStruct, pltpu.VMEM, pltpu.SemaphoreType.DMA
    return pl.pallas_call(
        functools.partial(reduce_kernel, n),
        out_shape=[S((FF, D), BF), S((D, FF), BF), S((D, D), BF), S((D, 3 * D), BF), S((16, CHUNK), F32)],
        in_specs=[ANY] * 8 + [VMEM] * 3,
        out_specs=[ANY] * 4 + [VMEM],
        scratch_shapes=[
            V((2, rows, T, CHUNK), BF), V((2, rows, T, CHUNK), BF), V((n_chunks, size, CHUNK // 2), BF),
            V((n_chunks, size, CHUNK // 2), BF),
            *[V((n_chunks, size >> (b + 1), CHUNK // 2), BF) for b in range(bits)],
            V((bits, 16, CHUNK), F32), V((2, CHUNK, CHUNK), BF), V((bits, 16, CHUNK), F32),
            DMA((2, 2)), DMA((2,)), DMA((n_chunks, bits)), DMA((n_chunks, bits)), DMA((n_chunks, bits)),
            DMA((n_chunks, bits)), DMA((bits,)), DMA((bits,)),
        ],
        compiler_params=pltpu.CompilerParams(vmem_limit_bytes=52 * 2**20, collective_id=0, has_side_effects=True),
        cost_estimate=pl.CostEstimate(flops=13 * 10**9, bytes_accessed=60 * 2**20, transcendentals=0),
        name="weight_grads",
    )(gelu, gl, second, ul, mixed, al, first, dproj, *vecs)


NONE = -4


def body(inputs, cotangent, lengths, norm1_gain, norm1_bias, weight_qkv, weight_out, bias_out, norm2_gain, norm2_bias,
         weight_up, bias_up, weight_down, bias_down):
    w = dict(n1g=norm1_gain, n1b=norm1_bias, wqkv=weight_qkv[0], wo=weight_out[0], bo=bias_out, n2g=norm2_gain,
             n2b=norm2_bias, wu=weight_up[0], bu=bias_up, wd=weight_down[0], bd=bias_down)
    x, cot = inputs[0], cotangent[0]
    n = lax.axis_size("dp")

    def ahead(block):
        return lax.ppermute(block, "section", [(0, 1)])

    def back(block):
        return lax.ppermute(block, "section", [(1, 0)])

    *kept_a, send_a = forward((0, NONE), lengths, x, x[0], w, [])
    row_0 = ahead(send_a)
    *kept_b, send_b = forward((1, 0), lengths, x, row_0, w, kept_a)
    row_1 = ahead(send_b)
    *grads_c, send_c, vec_c = backward((NONE, 0), lengths, x, row_0, cot, row_0, kept_b[1:], w, [])
    ret_0 = back(send_c)
    *kept_d, _ = forward((NONE, 1), lengths, x, row_1, w, kept_b)
    outputs, *saved = kept_d
    *grads_e, send_e, vec_e = backward((0, 1), lengths, x, row_1, cot, ret_0, saved, w, grads_c)
    ret_1 = back(send_e)
    *grads_g, _, vec_g = backward((1, NONE), lengths, x, row_1, cot, ret_1, saved, w, grads_e)
    wd, wu, wo, wqkv, vec = weight_grads(n, saved[1], grads_g, (vec_c, vec_e, vec_g))

    def wide(v):
        return v.astype(F32)[None]

    return (outputs[None], grads_g[0][None], vec[0:1], vec[1:2], wide(wqkv), wide(wo), vec[2:3], vec[3:4], vec[4:5],
            wide(wu), vec[6:10].reshape(1, -1), wide(wd), vec[5:6])


def solution(mesh):
    matrix, row = P("section", None, None), P("section", None)
    data = P("section", "dp", None, None)
    return jax.shard_map(
        body,
        mesh=mesh,
        in_specs=(data, data, P("dp", None), row, row, matrix, matrix, row, row, row, matrix, row, matrix, row),
        out_specs=(data, data, row, row, matrix, matrix, row, row, row, matrix, row, matrix, row),
        check_vma=False,
    )
```

time: 947 us -> 377 us (0.40)
  matrix products: 392 us -> 0 us
  Pallas kernels: 0 us -> 245 us
  other arithmetic: 164 us -> 8.32 us
  local copies, waits for them, and re-layouts: 110 us -> 7.98 us
  waiting for transfers between devices: 181 us -> 104 us
  blocking collectives: 61.1 us -> 0 us
  between operations: 17.3 us -> 1.27 us
    dot_general x72 -> x0, matrix products: 392 us -> none  [the longest x6 64.8 us: attend_backward(): jnp.einsum('bqhd,bkhd->bhqk', block_out, values_all, preferred_element_ty...]
    pallas_call x0 -> x7, Pallas kernels: none -> 245 us  [the longest x1 110 us: weight_grads(): pl.pallas_call(functools.partial(reduce_kernel, n), out_shape=[S((FF, D),...]
    psum x1 -> x0, waiting for transfers between devices: 134 us -> none  [body(): lax.psum((pending[0], pending[1], pending[2], pending[3], pending[4], pen...]
    convert_element_type x9 -> x0, other arithmetic: 81.4 us -> none  [the longest x6 77 us: attend_backward(): score_grad = (probs * (prob_grad - inner)).astype(jnp.bfloat16)]
    reduce_sum x31 -> x0, other arithmetic: 67 us -> none  [the longest x6 30.1 us: attend_forward(): total = jnp.sum(raised, -1, keepdims=True)]
    psum x1 -> x0, blocking collectives: 61.1 us -> none  [body(): lax.psum((pending[0], pending[1], pending[2], pending[3], pending[4], pen...]
    ppermute x4, waiting for transfers between devices: 47 us -> 104 us  [the longest x2 64.9 us: back(): return lax.ppermute(block, 'section', [(1, 0)])]
    unnamed x496 -> x62, local copies, waits for them, and re-layouts: 58.6 us -> 5.94 us
  transfers between devices with their start and end apart: 5 -> 4, of which waited for: 5 -> 4; matrix products, arithmetic and copies ran while one was open for 9% -> 0% of each run, Pallas kernels for 0% -> 1%
where the time goes in v1:
time: 377 us; the launch traced here: 376 us
  Pallas kernels  245 us (65%)
  waiting for transfers between devices  104 us (28%)
  starting transfers between devices  9.16 us (2%)
  other arithmetic  8.32 us (2%)
  local copies, waits for them, and re-layouts  7.98 us (2%)
    pallas_call x1, Pallas kernels, weight_grads(): pl.pallas_call(functools.partial(reduce_kernel, n), out_shape=[S((FF, D),...  110 us
    pallas_call x3, Pallas kernels, backward(): pl.pallas_call(functools.partial(backward_kernel, rows_of), out_shape=out...  76.6 us
    ppermute x2, waiting for transfers between devices, back(): return lax.ppermute(block, 'section', [(1, 0)])  64.9 us
    pallas_call x3, Pallas kernels, forward(): pl.pallas_call(functools.partial(forward_kernel, rows_of), out_shape=outs...  58.9 us
    ppermute x2, waiting for transfers between devices, ahead(): return lax.ppermute(block, 'section', [(0, 1)])  38.9 us
    broadcast_in_dim x4, other arithmetic, wide(): return v.astype(F32)[None]  8.32 us
  transfers between devices with their start and end apart: 4, of which 4 were waited for; matrix products, arithmetic and copies ran while one was open for 0% of the time, Pallas kernels for 1%

profile of v1, /device:TPU:0, one launch (start us, length us, event | category | flops | bytes accessed | tf_op | source)
XLA Modules:
  0.0 375.8 jit_solution(1122724630771091531)
XLA Ops:
  0.6 0.0 copy-start.12
  0.7 0.0 copy-start.10
  0.7 0.0 copy-start.8
  0.7 0.0 copy-start.6
  0.7 0.0 copy-start.16
  0.7 0.0 copy-start.3
  0.7 0.0 copy-start
  0.7 1.4 slice_bitcast_fusion.refs_2_
  2.2 0.4 copy-done
  2.6 0.7 copy-done.14
  3.3 0.7 copy-done.18
  4.0 0.7 copy-done.20
  4.7 23.8 %row_forward.3 = (bf16[2,1024,512]{2,1,0:T(8,128)(2,1)}, bf16[2,1024,1536]{2,1,0:T(8,128)(2,1)}, bf16[2,1024,512]{2,1,0:T(8,128)(2,1)}, f32[2,1024,512]{2,1,0:T(...) custom-call(s32[2,8]{1,0:T(2,128)S(1)} %copy-done.16, bf16[2,1024,512]{2,1,0:T(8,128)(2,1)} %bitcast.38, ...), custom_call_target="tpu_custom_call" | custom-call | flops 8000000000 | bytes 20971520 | tf_op jit(solution)/shard_map/row_forward/pallas_call | solution.py:205
  28.5 1.4 collective-permute-start
  29.9 22.2 %collective-permute-done.refs_2_.refs_4_ = bf16[1024,512]{1,0:T(8,128)(2,1)S(1)} collective-permute-done((bf16[1024,512]{1,0:T(8,128)(2,1)S(1)}, bf16[1024,512]{1,0:T(8,128)(2,1)S(1)}, u32[]{:S(2)}, u32[]{:S(2)}) %collective-permute-start) | collective-permute-done | bytes 1048608 | tf_op jit(solution)/shard_map/ppermute | solution.py:630
  52.1 34.2 %row_forward.4 = (bf16[2,1024,512]{2,1,0:T(8,128)(2,1)}, bf16[2,1024,1536]{2,1,0:T(8,128)(2,1)}, bf16[2,1024,512]{2,1,0:T(8,128)(2,1)}, f32[2,1024,512]{2,1,0:T(...) custom-call(s32[2,8]{1,0:T(2,128)S(1)} %copy-done.16, ...), custom_call_target="tpu_custom_call", output_to_operand_aliasing={{0}: (14, {}), {1}: (15, {}), {2}: (16, {}), {3}: (17, {}),... | custom-call | flops 8000000000 | bytes 20971520 | tf_op jit(solution)/shard_map/row_forward/pallas_call | solution.py:205
  86.3 5.2 %collective-permute-start.1 = (bf16[1024,512]{1,0:T(8,128)(2,1)S(1)}, bf16[1024,512]{1,0:T(8,128)(2,1)S(1)}, u32[]{:S(2)}, u32[]{:S(2)}) collective-permute-start(bf16[1024,512]{1,0:T(8,128)(2,1)S(1)} %get-tuple-element.70), channel_id=1, source_target_pairs={{0,16},{1,17},{2,18},{3,19},{4,20},{5,21},{6,22},{7,23},{8,24},{9,... | collective-permute-start | bytes 3145736 | tf_op jit(solution)/shard_map/ppermute | solution.py:630
  91.6 0.0 copy-start.1
  91.6 0.0 copy-start.4
  91.6 0.0 copy-start.7
  91.6 0.0 copy-start.9
  91.6 0.0 copy-start.11
  91.6 0.0 copy-start.13
  91.6 0.0 copy-start.15
  91.6 0.0 copy-start.17
  91.7 0.0 copy-start.19
  91.7 0.0 copy-start.21
  91.7 2.1 row_backward.3
  93.8 1.3 collective-permute-start.2
  95.1 16.7 %collective-permute-done.1.refs_2_ = bf16[1024,512]{1,0:T(8,128)(2,1)S(1)} collective-permute-done((bf16[1024,512]{1,0:T(8,128)(2,1)S(1)}, bf16[1024,512]{1,0:T(8,128)(2,1)S(1)}, u32[]{:S(2)}, u32[]{:S(2)}) %collective-permute-start.1) | collective-permute-done | bytes 1048608 | tf_op jit(solution)/shard_map/ppermute | solution.py:630
  111.9 0.8 row_forward.5
  112.8 0.0 copy-done.2
  112.8 39.4 %collective-permute-done.2.refs_4_ = bf16[1024,512]{1,0:T(8,128)(2,1)S(1)} collective-permute-done((bf16[1024,512]{1,0:T(8,128)(2,1)}, bf16[1024,512]{1,0:T(8,128)(2,1)S(1)}, u32[]{:S(2)}, u32[]{:S(2)}) %collective-permute-start.2) | collective-permute-done | bytes 1048608 | tf_op jit(solution)/shard_map/ppermute | solution.py:633
  152.2 1.0 copy-done.28
  153.2 37.1 %row_backward.4 = (f32[2,1024,512]{2,1,0:T(8,128)}, bf16[2,1024,512]{2,1,0:T(8,128)(2,1)}, bf16[2,1024,1536]{2,1,0:T(8,128)(2,1)}, bf16[2,1024,512]{2,1,0:T(8,12...) custom-call(s32[2,8]{1,0:T(2,128)} %refs_0_.11, ...), custom_call_target="tpu_custom_call", output_to_operand_aliasing={{0}: (16, {}), {1}: (17, {}), {2}: (18, {}), {3}: (19, {}),... | custom-call | flops 14000000000 | bytes 38797312 | tf_op jit(solution)/shard_map/row_backward/pallas_call | solution.py:394
  190.3 1.3 collective-permute-start.3
  191.6 25.5 %collective-permute-done.3.refs_4_ = bf16[1024,512]{1,0:T(8,128)(2,1)S(1)} collective-permute-done((bf16[1024,512]{1,0:T(8,128)(2,1)}, bf16[1024,512]{1,0:T(8,128)(2,1)S(1)}, u32[]{:S(2)}, u32[]{:S(2)}) %collective-permute-start.3) | collective-permute-done | bytes 1048608 | tf_op jit(solution)/shard_map/ppermute | solution.py:633
  217.1 1.0 copy-done.29
  218.1 37.3 %row_backward.5 = (f32[2,1024,512]{2,1,0:T(8,128)}, bf16[2,1024,512]{2,1,0:T(8,128)(2,1)}, bf16[2,1024,1536]{2,1,0:T(8,128)(2,1)}, bf16[2,1024,512]{2,1,0:T(8,12...) custom-call(s32[2,8]{1,0:T(2,128)} %refs_0_.11, ...), custom_call_target="tpu_custom_call", output_to_operand_aliasing={{0}: (16, {}), {1}: (17, {}), {2}: (18, {}), {3}: (19, {}),... | custom-call | flops 14000000000 | bytes 38797312 | tf_op jit(solution)/shard_map/row_backward/pallas_call | solution.py:394
  255.4 0.7 copy-done.23
  256.2 109.7 %weight_grads.1 = (bf16[2048,512]{1,0:T(8,128)(2,1)}, bf16[512,2048]{1,0:T(8,128)(2,1)}, bf16[512,512]{1,0:T(8,128)(2,1)S(1)}, bf16[512,1536]{1,0:T(8,128)(2,1)}, f32[16,512]{1,0:T(8,128)S(1)}) custom-call(bf16[2,1024,2048]{2,1,0:T(8,128)(2,1)} %get-tuple-element.99.refs_0_, bf16[2,1024,512]{2,1,0:T(8,128)(2,1)} %get-tuple-element.100.refs_1_, ...), custom_call_target="tpu_custom_call" | custom-call | flops 12999999488 | bytes 62914560 | tf_op jit(solution)/shard_map/weight_grads/pallas_call | solution.py:600
  366.0 0.6 fusion
  366.6 0.6 copy.53
  367.2 1.1 bitcast_convert_fusion.3
  368.3 2.1 bitcast_convert_fusion.2
  370.3 0.0 copy-done.26
  370.4 2.5 bitcast_convert_fusion.1
  372.9 2.6 bitcast_convert_fusion
  (35 shorter events, 0.1 us)
Async XLA Ops:
  0.6 1.5 copy-start.12
  0.7 1.5 copy-start.10
  0.7 1.5 copy-start.8
  0.7 1.5 copy-start.6
  0.7 1.5 copy-start.16
  0.7 1.5 copy-start.3
  0.7 1.9 copy-start
  2.6 0.7 copy-start.14
  3.3 0.7 copy-start.18
  4.0 0.7 copy-start.20
  28.5 23.6 %collective-permute-start = (bf16[1024,512]{1,0:T(8,128)(2,1)S(1)}, bf16[1024,512]{1,0:T(8,128)(2,1)S(1)}, u32[]{:S(2)}, u32[]{:S(2)}) collective-permute-start(bf16[1024,512]{1,0:T(8,128)(2,1)S(1)} %get-tuple-element.64), channel_id=1, source_target_pairs={{0,16},{1,17},{2,18},{3,19},{4,20},{5,21},{6,22},{7,23},{8,24},{9,... | collective-permute-start | bytes 3145736 | tf_op jit(solution)/shard_map/ppermute | solution.py:630
  52.1 34.3 %copy-start.5 = (bf16[1024,512]{1,0:T(8,128)(2,1)}, bf16[1024,512]{1,0:T(8,128)(2,1)S(1)}, u32[]{:S(2)}) copy-start(bf16[1024,512]{1,0:T(8,128)(2,1)S(1)} %collective-permute-done.refs_2_.refs_4_) | copy-start | bytes 3145732
  86.3 25.5 %collective-permute-start.1 = (bf16[1024,512]{1,0:T(8,128)(2,1)S(1)}, bf16[1024,512]{1,0:T(8,128)(2,1)S(1)}, u32[]{:S(2)}, u32[]{:S(2)}) collective-permute-start(bf16[1024,512]{1,0:T(8,128)(2,1)S(1)} %get-tuple-element.70), channel_id=1, source_target_pairs={{0,16},{1,17},{2,18},{3,19},{4,20},{5,21},{6,22},{7,23},{8,24},{9,... | collective-permute-start | bytes 3145736 | tf_op jit(solution)/shard_map/ppermute | solution.py:630
  91.6 20.3 %copy-start.1 = (bf16[1,512,1536]{2,1,0:T(8,128)(2,1)S(1)}, bf16[1,512,1536]{2,1,0:T(8,128)(2,1)}, u32[]{:S(2)}) copy-start(bf16[1,512,1536]{2,1,0:T(8,128)(2,1)} %param.19) | copy-start | bytes 4718596
  91.6 20.2 %copy-start.4 = (bf16[1,512,512]{2,1,0:T(8,128)(2,1)S(1)}, bf16[1,512,512]{2,1,0:T(8,128)(2,1)}, u32[]{:S(2)}) copy-start(bf16[1,512,512]{2,1,0:T(8,128)(2,1)} %param.20) | copy-start | bytes 1572868
  91.6 20.2 %copy-start.7 = (f32[1,512]{1,0:T(1,128)S(1)}, f32[1,512]{1,0:T(1,128)}, u32[]{:S(2)}) copy-start(f32[1,512]{1,0:T(1,128)} %refs_12_.11) | copy-start | bytes 6148
  91.6 20.2 %copy-start.9 = (f32[1,512]{1,0:T(1,128)S(1)}, f32[1,512]{1,0:T(1,128)}, u32[]{:S(2)}) copy-start(f32[1,512]{1,0:T(1,128)} %refs_13_.11) | copy-start | bytes 6148
  91.6 20.2 %copy-start.11 = (f32[1,512]{1,0:T(1,128)S(1)}, f32[1,512]{1,0:T(1,128)}, u32[]{:S(2)}) copy-start(f32[1,512]{1,0:T(1,128)} %refs_14_.5) | copy-start | bytes 6148
  91.6 20.2 %copy-start.13 = (f32[1,512]{1,0:T(1,128)S(1)}, f32[1,512]{1,0:T(1,128)}, u32[]{:S(2)}) copy-start(f32[1,512]{1,0:T(1,128)} %refs_15_.5) | copy-start | bytes 6148
  91.6 20.2 %copy-start.15 = (f32[1,2048]{1,0:T(1,128)S(1)}, f32[1,2048]{1,0:T(1,128)}, u32[]{:S(2)}) copy-start(f32[1,2048]{1,0:T(1,128)} %refs_12_.8) | copy-start | bytes 24580
  91.6 20.2 %copy-start.17 = (s32[2,8]{1,0:T(2,128)S(1)}, s32[2,8]{1,0:T(2,128)}, u32[]{:S(2)}) copy-start(s32[2,8]{1,0:T(2,128)} %refs_0_.11) | copy-start | bytes 196
  91.7 20.2 %copy-start.19 = (f32[1,512]{1,0:T(1,128)S(1)}, f32[1,512]{1,0:T(1,128)}, u32[]{:S(2)}) copy-start(f32[1,512]{1,0:T(1,128)} %refs_9_.5) | copy-start | bytes 6148
  91.7 20.2 %copy-start.21 = (f32[1,512]{1,0:T(1,128)S(1)}, f32[1,512]{1,0:T(1,128)}, u32[]{:S(2)}) copy-start(f32[1,512]{1,0:T(1,128)} %refs_13_.8) | copy-start | bytes 6148
  93.8 58.4 %collective-permute-start.2 = (bf16[1024,512]{1,0:T(8,128)(2,1)}, bf16[1024,512]{1,0:T(8,128)(2,1)S(1)}, u32[]{:S(2)}, u32[]{:S(2)}) collective-permute-start(bf16[1024,512]{1,0:T(8,128)(2,1)} %get-tuple-element.77), channel_id=1, source_target_pairs={{16,0},{17,1},{18,2},{19,3},{20,4},{21,5},{22,6},{23,7},{24,8},{25... | collective-permute-start | bytes 3145736 | tf_op jit(solution)/shard_map/ppermute | solution.py:633
  111.8 1.0 copy-start.2
  152.2 1.0 copy-start.28
  190.3 26.8 %collective-permute-start.3 = (bf16[1024,512]{1,0:T(8,128)(2,1)}, bf16[1024,512]{1,0:T(8,128)(2,1)S(1)}, u32[]{:S(2)}, u32[]{:S(2)}) collective-permute-start(bf16[1024,512]{1,0:T(8,128)(2,1)} %get-tuple-element.89), channel_id=1, source_target_pairs={{16,0},{17,1},{18,2},{19,3},{20,4},{21,5},{22,6},{23,7},{24,8},{25... | collective-permute-start | bytes 3145736 | tf_op jit(solution)/shard_map/ppermute | solution.py:633
  217.1 1.0 copy-start.29
  218.1 37.3 %copy-start.22 = (f32[16,512]{1,0:T(8,128)S(1)}, f32[16,512]{1,0:T(8,128)}, u32[]{:S(2)}) copy-start(f32[16,512]{1,0:T(8,128)} %get-tuple-element.108.refs_9_) | copy-start | bytes 98308
  218.1 37.3 %copy-start.24 = (f32[16,512]{1,0:T(8,128)S(1)}, f32[16,512]{1,0:T(8,128)}, u32[]{:S(2)}) copy-start(f32[16,512]{1,0:T(8,128)} %get-tuple-element.107.refs_8_) | copy-start | bytes 98308
  255.4 0.8 copy-start.23
  365.9 2.3 copy-start.27
  368.3 2.1 copy-start.26
  370.4 2.5 copy-start.25

commit v2 on v1

v2 whole, which is shorter than its diff:
```python
import functools

import jax
import jax.numpy as jnp
from jax import lax
from jax.experimental import pallas as pl
from jax.experimental.pallas import tpu as pltpu
from jax.sharding import PartitionSpec as P

EPSILON = 1e-05
GELU_C = 0.7978845608028654
MASKED = -1e30
TILE = 512
CHUNK = 512
NONE = -4
BF = jnp.bfloat16
F32 = jnp.float32
MESH = pl.DeviceIdType.MESH
ANY = pl.BlockSpec(memory_space=pl.ANY)
VMEM = pl.BlockSpec(memory_space=pltpu.VMEM)
SMEM = pl.BlockSpec(memory_space=pltpu.SMEM)


def dot(a, b):
    return jnp.dot(a, b, preferred_element_type=F32)


def dot_nt(a, b):
    return lax.dot_general(a, b, (((1,), (1,)), ((), ())), preferred_element_type=F32)


def dot_tn(a, b):
    return lax.dot_general(a, b, (((0,), (0,)), ((), ())), preferred_element_type=F32)


def norm_parts(v):
    centred = v - jnp.mean(v, -1, keepdims=True)
    rstd = lax.rsqrt(jnp.mean(centred * centred, -1, keepdims=True) + EPSILON)
    return centred * rstd, rstd


def norm_pull(grad, hat, rstd, gain):
    scaled = grad * gain
    return rstd * (
        scaled
        - jnp.mean(scaled, -1, keepdims=True)
        - hat * jnp.mean(scaled * hat, -1, keepdims=True)
    )


def colsum(v):
    return jnp.sum(v, 0, keepdims=True)


def stack_pair(block):
    lane = lax.broadcasted_iota(jnp.int32, block.shape, 1)
    zero = jnp.zeros_like(block)
    low = lane < 64
    return jnp.concatenate([jnp.where(low, block, zero), jnp.where(low, zero, block)], 0)


def unstack_pair(both):
    rows = both.shape[0] // 2
    lane = lax.broadcasted_iota(jnp.int32, (rows, 128), 1)
    return jnp.where(lane < 64, both[:rows], both[rows:])


def tile_rows(t):
    return pl.ds(pl.multiple_of(t * TILE, TILE), TILE)


def for_spans(lengths, row, length, run):
    def body(s, first):
        last = first + lengths[row, s]
        base = (first // 16) * 16
        need = last - base

        def keep_of(window, low, high):
            def keep(width):
                pos = lax.broadcasted_iota(jnp.int32, (window, width), 0)
                return (pos >= low) & (pos < high)

            return keep

        def put(ref, rows, cols, keep, value):
            ref[rows, cols] = jnp.where(keep, value.astype(BF), ref[rows, cols])

        def case(above, window):
            @pl.when((need > above) & (need <= window))
            def _():
                start = pl.multiple_of(jnp.minimum(base, length - window), 16)
                rows = pl.ds(start, window)
                keep = keep_of(window, first - start, last - start)
                run(lambda ref, cols: ref[rows, cols],
                    lambda ref, cols, value: put(ref, rows, cols, keep(128), value), keep, window)

        case(0, 128)
        case(128, 256)

        @pl.when(need > 256)
        def _():
            start = pl.multiple_of(base, 16)
            shift = first - base
            rows = pl.ds(start, 272)

            def load(ref, cols):
                return pltpu.roll(ref[rows, cols].astype(F32), 272 - shift, 0)[:256].astype(BF)

            def store(ref, cols, value):
                wide = jnp.concatenate([value.astype(F32), jnp.zeros((16, value.shape[1]), F32)], 0)
                put(ref, rows, cols, keep_of(272, shift, last - base)(128), pltpu.roll(wide, shift, 0))

            run(load, store, keep_of(256, 0, last - first), 256)

        return last

    lax.fori_loop(0, lengths.shape[1], body, 0)


def pick(pair):
    return pair[0] + lax.axis_index("section") * (pair[1] - pair[0])


def row_kernel(f_rows, b_rows, names, *refs):
    r = dict(zip(names, refs))
    lengths = r["lengths"]
    fused = b_rows[1] >= 0
    both = f_rows[0] >= 0 and f_rows[1] >= 0
    with_arr = f_rows[1] >= 0
    v_x = r["v_x"]
    T, D = v_x.shape
    FF = r["w_up"].shape[1]
    n_tiles = T // TILE
    sem_in, sem_out = r["sem_in"], r["sem_out"]
    section = lax.axis_index("section")
    v_proj, v_att, v_up = r["v_proj"], r["v_att"], r["v_up"]
    w_qkv, w_out, w_up, w_down = r["w_qkv"], r["w_out"], r["w_up"], r["w_down"]
    ins, outs = {}, {}

    def load(key, source, target):
        k = ins.setdefault(key, len(ins))
        return pltpu.make_async_copy(source, target, sem_in.at[k])

    def load_tile(key, source, target, t):
        return load((key, t), source.at[tile_rows(t)], target.at[tile_rows(t)])

    def sends(t, pairs):
        rows = tile_rows(t)
        copies = []
        for key, source, target in pairs:
            k = outs.setdefault(key, len(outs))
            copies.append(pltpu.make_async_copy(source.at[rows], target.at[rows], sem_out.at[k, t]))
        return copies

    if "vec" in r:
        r["vec"][...] = jnp.zeros_like(r["vec"])

    def hidden(rows):
        h = v_x[rows, :].astype(F32)
        return h + r["v_arr"][rows, :].astype(F32) if with_arr else h

    def forward(row):
        c_x = [load_tile("x", r["x"].at[row], v_x, t) for t in range(n_tiles)]
        c_qkv = load("wqkv", r["wqkv"], w_qkv)
        later = [load("wo", r["wo"], w_out), load("wu", r["wu"], w_up), load("wd", r["wd"], w_down)]
        for c in c_x + [c_qkv]:
            c.start()
        if with_arr:
            c_arr = [load_tile("arr", r["arr"], r["v_arr"], t) for t in range(n_tiles)]

            @pl.when(section == 1)
            def _():
                for c in c_arr:
                    c.start()

            if both:
                @pl.when(section == 0)
                def _():
                    r["v_arr"][...] = jnp.zeros_like(r["v_arr"])
        for c in later:
            c.start()
        if fused:
            @pl.when(section == 1)
            def _():
                for t in range(n_tiles):
                    load_tile("cot", r["cot"].at[row], r["v_cot"], t).start()
        v_mixed = r["v_mixed"]
        pairs_a = [("proj", v_proj, r["proj"].at[row])] if f_rows[0] >= 0 else []
        pairs_b = [("out", r["v_out"], r["out"].at[row])]
        pairs_c = []
        if f_rows[0] >= 0:
            pairs_c = [("snd", r["v_out"], r["snd"]), ("att", v_att, r["att"].at[row]), ("up", v_up, r["up"].at[row])]

        def keep_for_encoder(t, pairs, act):
            if pairs:
                @pl.when(section == 0)
                def _():
                    for c in sends(t, pairs):
                        act(c)

        for t in range(n_tiles):
            c_x[t].wait()
            if with_arr:
                @pl.when(section == 1)
                def _():
                    c_arr[t].wait()
            if t == 0:
                c_qkv.wait()
            rows = pl.ds(t * TILE, TILE)
            first = (norm_parts(hidden(rows))[0] * r["n1g"][...] + r["n1b"][...]).astype(BF)
            v_proj[rows, :] = dot(first, w_qkv[...]).astype(BF)
            keep_for_encoder(t, pairs_a, lambda c: c.start())

        def run(load, store, keep, window):
            kmask = jnp.where(keep(128), 0.0, MASKED)
            pairs = range(D // 128)
            q = [stack_pair(load(v_proj, slice(p * 128, p * 128 + 128)) * jnp.asarray(0.125, BF)) for p in pairs]
            k = [load(v_proj, slice(D + p * 128, D + p * 128 + 128)) for p in pairs]
            v = [load(v_proj, slice(2 * D + p * 128, 2 * D + p * 128 + 128)) for p in pairs]
            score = [dot_nt(k[p], q[p]) for p in pairs]
            raised, sums = [], []
            for p in pairs:
                parts = []
                for j in range(0, 2 * window, 128):
                    block = score[p][:, j:j + 128] + kmask
                    e = jnp.exp(block - jnp.max(block, 0, keepdims=True))
                    sums.append(jnp.sum(e, 0, keepdims=True))
                    parts.append(e.astype(BF))
                raised.append(jnp.concatenate(parts, 1))
            outs = [dot_tn(v[p], raised[p]) for p in pairs]
            blocks = 2 * window // 128
            for p in pairs:
                o = outs[p] * (1.0 / jnp.concatenate(sums[p * blocks:(p + 1) * blocks], 1))
                o = jnp.concatenate([o[:64, :window], o[64:, window:]], 0).T
                store(v_mixed, slice(p * 128, p * 128 + 128), o)

        for_spans(lengths, row, T, run)
        c_mixed = pltpu.make_async_copy(v_mixed, r["mixed"].at[row], r["sem_mixed"].at[0])
        c_mixed.start()
        for c in later:
            c.wait()

        def post_tile(t, carry):
            rows = tile_rows(t)
            a = hidden(rows) + dot(v_mixed[rows, :], w_out[...]) + r["bo"][...]
            v_att[rows, :] = a
            second = (norm_parts(a)[0] * r["n2g"][...] + r["n2b"][...]).astype(BF)
            u = dot(second, w_up[...]) + r["bu"][...]
            v_up[rows, :] = u.astype(BF)
            g = jax.nn.gelu(u, approximate=True).astype(BF)
            r["v_out"][rows, :] = (a + r["bd"][...] + dot(g, w_down[...])).astype(BF)
            for c in sends(t, pairs_b):
                c.start()
            keep_for_encoder(t, pairs_c, lambda c: c.start())
            return carry

        lax.fori_loop(0, n_tiles, post_tile, 0)

        def finish():
            c_mixed.wait()
            for t in range(n_tiles):
                for c in sends(t, pairs_b):
                    c.wait()
                keep_for_encoder(t, pairs_a + pairs_c, lambda c: c.wait())

        return finish

    def backward(row):
        v_cot, v_gl, v_ul, v_second, v_al = [r["v_" + k] for k in ("cot", "gl", "ul", "second", "al")]
        v_da, v_dmix, v_dproj, v_first, v_dh, vec = [r[k] for k in ("v_da", "v_dmix", "v_dproj", "v_first", "v_dh", "vec")]
        if not fused:
            c_wd = load("wd", r["wd"], w_down)
            c_wu = load("wu", r["wu"], w_up)
            c_wo = load("wo", r["wo"], w_out)
            c_att = load("att", r["att"].at[row], v_att)
            late = [load("proj", r["proj"].at[row], v_proj), load("wqkv", r["wqkv"], w_qkv), load("x", r["x"].at[row], v_x)]

            def tile_loads(t):
                return [load_tile("cot", r["cot"].at[row], v_cot, t), load_tile("ret", r["ret"], r["v_ret"], t),
                        load_tile("up", r["up"].at[row], v_up, t)]

            for c in tile_loads(0) + [c_wd, c_wu, c_att, c_wo]:
                c.start()
            for t in range(1, n_tiles):
                for c in tile_loads(t):
                    c.start()
            for c in late:
                c.start()

        pairs_a = [("gl", v_gl, r["gl"].at[row]), ("gelu", v_up, r["gelu"].at[row]), ("ul", v_ul, r["ul"].at[row]),
                   ("second", v_second, r["second"].at[row]), ("al", v_al, r["al"].at[row])]
        pairs_b = [("first", v_first, r["first"].at[row]), ("dproj", v_dproj, r["dproj"].at[row]),
                   ("dh", v_dh, r["dh"].at[row])]
        if fused:
            pairs_b.append(("bsnd", r["v_bsnd"], r["bsnd"]))
        text_end = T - lengths[row, lengths.shape[1] - 1]

        def pre_tile(t):
            rows = pl.ds(t * TILE, TILE)
            if fused:
                load_tile("cot", r["cot"].at[row], v_cot, t).wait()
            else:
                for c in tile_loads(t):
                    c.wait()
                if t == 0:
                    c_wd.wait()
            pos = t * TILE + lax.broadcasted_iota(jnp.int32, (TILE, 1), 0)
            in_text = (pos < text_end).astype(F32)
            g = v_cot[rows, :].astype(F32) * in_text
            if not fused:
                g = g + r["v_ret"][rows, :].astype(F32)
            g_low = g.astype(BF)
            v_gl[rows, :] = g_low
            vec[5:6, :] += colsum(g)
            sg = jnp.zeros((TILE, D), F32)
            for c in range(0, FF, CHUNK):
                cc = slice(c, c + CHUNK)
                u = v_up[rows, cc].astype(F32)
                uu = u * u
                th = jnp.tanh(u * (GELU_C + (GELU_C * 0.044715) * uu))
                half = 0.5 * (1.0 + th)
                v_up[rows, cc] = (u * half).astype(BF)
                slope = half + (0.5 * u) * (1.0 - th * th) * (GELU_C + (3.0 * GELU_C * 0.044715) * uu)
                ug = dot_nt(g_low, w_down[cc, :]) * slope
                vec[6 + c // CHUNK:7 + c // CHUNK, :] += colsum(ug)
                ug_low = ug.astype(BF)
                v_ul[rows, cc] = ug_low
                if not fused and t == 0 and c == 0:
                    c_wu.wait()
                sg = sg + dot_nt(ug_low, w_up[:, cc])
            if not fused and t == 0:
                c_att.wait()
                c_wo.wait()
            hat, rstd = norm_parts(v_att[rows, :])
            v_second[rows, :] = (hat * r["n2g"][...] + r["n2b"][...]).astype(BF)
            vec[3:4, :] += colsum(sg * hat)
            vec[4:5, :] += colsum(sg)
            a = g + norm_pull(sg, hat, rstd, r["n2g"][...])
            vec[2:3, :] += colsum(a)
            v_da[rows, :] = a
            a_low = a.astype(BF)
            v_al[rows, :] = a_low
            v_dmix[rows, :] = dot_nt(a_low, w_out[...]).astype(BF)
            for c in sends(t, pairs_a):
                c.start()

        for t in range(n_tiles):
            pre_tile(t)
        if not fused:
            late[0].wait()

        def run(load, store, keep, window):
            kmask = jnp.where(keep(128), 0.0, MASKED)
            inside = keep(128)
            zero = jnp.zeros((window, 128), BF)
            eighth = jnp.asarray(0.125, BF)
            pairs = range(D // 128)

            def cols(third, p):
                return slice(third * D + p * 128, third * D + p * 128 + 128)

            q = [stack_pair(load(v_proj, cols(0, p)) * eighth) for p in pairs]
            k = [load(v_proj, cols(1, p)) for p in pairs]
            v = [load(v_proj, cols(2, p)) for p in pairs]
            do = [stack_pair(jnp.where(inside, load(v_dmix, cols(0, p)), zero)) for p in pairs]
            score = [dot_nt(k[p], q[p]) for p in pairs]
            pulls = [dot_nt(v[p], do[p]) for p in pairs]
            def soft(p):
                prob_parts, ds_parts = [], []
                for j in range(0, 2 * window, 128):
                    block = score[p][:, j:j + 128] + kmask
                    e = jnp.exp(block - jnp.max(block, 0, keepdims=True))
                    prob = e * (1.0 / jnp.sum(e, 0, keepdims=True))
                    pull = pulls[p][:, j:j + 128]
                    inner = jnp.sum(pull * prob, 0, keepdims=True)
                    ds_parts.append((prob * (pull - inner)).astype(BF))
                    prob_parts.append(prob.astype(BF))
                return jnp.concatenate(prob_parts, 1), jnp.concatenate(ds_parts, 1)

            def mix(p, prob, push):
                store(v_dproj, cols(2, p), dot(prob, do[p]))
                store(v_dproj, cols(1, p), dot(push, q[p]))
                dq = dot_tn(k[p] * eighth, push)
                store(v_dproj, cols(0, p), jnp.concatenate([dq[:64, :window], dq[64:, window:]], 0).T)

            ahead = soft(0)
            for p in pairs:
                now = ahead
                if p + 1 < len(pairs):
                    ahead = soft(p + 1)
                mix(p, *now)

        for_spans(lengths, row, T, run)
        if not fused:
            late[1].wait()
            late[2].wait()

        def fin_tile(t, carry):
            rows = tile_rows(t)
            fg = dot_nt(v_dproj[rows, :], w_qkv[...])
            hat, rstd = norm_parts(hidden(rows))
            v_first[rows, :] = (hat * r["n1g"][...] + r["n1b"][...]).astype(BF)
            vec[0:1, :] += colsum(fg * hat)
            vec[1:2, :] += colsum(fg)
            d = v_da[rows, :] + norm_pull(fg, hat, rstd, r["n1g"][...])
            v_dh[rows, :] = d
            if fused:
                r["v_bsnd"][rows, :] = d.astype(BF)
            for c in sends(t, pairs_b):
                c.start()
            return carry

        lax.fori_loop(0, n_tiles, fin_tile, 0)
        for t in range(n_tiles):
            for c in sends(t, pairs_a) + sends(t, pairs_b):
                c.wait()

    if f_rows != (NONE, NONE):
        f_row = pick(f_rows)

        @pl.when(f_row >= 0)
        def _():
            finish = forward(f_row)
            if fused:
                @pl.when(section == 1)
                def _():
                    backward(f_row)
            finish()
    else:
        b_row = pick(b_rows)

        @pl.when(b_row >= 0)
        def _():
            backward(b_row)


def row_slot(f_rows, b_rows, lengths, x, cot, arr, ret, w, bufs):
    n, T, D = x.shape
    FF = w["wu"].shape[1]
    S, V = jax.ShapeDtypeStruct, pltpu.VMEM
    does_f, does_b = max(f_rows) >= 0, max(b_rows) >= 0
    saves = f_rows[0] >= 0
    fused = b_rows[1] >= 0
    ins = {"lengths": (lengths, SMEM), "x": (x, ANY)}
    if does_b:
        ins["cot"] = (cot, ANY)
    if arr is not None:
        ins["arr"] = (arr, ANY)
    if ret is not None:
        ins["ret"] = (ret, ANY)
        ins.update({k: (bufs[k], ANY) for k in ("proj", "att", "up")})
    ins.update({k: (w[k], ANY) for k in ("wqkv", "wo", "wu", "wd")})
    ins.update({k: (w[k], VMEM) for k in ("n1g", "n1b", "bo", "n2g", "n2b", "bu", "bd")})
    wide = {"out": (D, BF), "mixed": (D, BF), "proj": (3 * D, BF), "att": (D, F32), "up": (FF, BF), "dh": (D, F32),
            "first": (D, BF), "dproj": (3 * D, BF), "al": (D, BF), "second": (D, BF), "ul": (FF, BF), "gelu": (FF, BF),
            "gl": (D, BF)}
    keys = (["out", "mixed"] if does_f else []) + (["proj", "att", "up"] if saves else [])
    if does_b:
        keys += ["dh", "first", "dproj", "al", "second", "ul", "gelu", "gl"]
    outs = {k: (S((n, T, wide[k][0]), wide[k][1]), ANY) for k in keys}
    if saves:
        outs["snd"] = (S((T, D), BF), ANY)
    if fused:
        outs["bsnd"] = (S((T, D), BF), ANY)
    if does_b:
        outs["vec"] = (S((16, CHUNK), F32), VMEM)
    alias = [k for k in keys if k in bufs]
    scratch = {"v_x": V((T, D), BF), "w_qkv": V((D, 3 * D), BF), "w_out": V((D, D), BF), "w_up": V((D, FF), BF),
               "w_down": V((FF, D), BF), "v_proj": V((T, 3 * D), BF), "v_att": V((T, D), F32), "v_up": V((T, FF), BF)}
    if arr is not None:
        scratch["v_arr"] = V((T, D), BF)
    if ret is not None:
        scratch["v_ret"] = V((T, D), BF)
    if does_f:
        scratch.update({"v_mixed": V((T, D), BF), "v_out": V((T, D), BF)})
    if does_b:
        scratch.update({"v_" + k: V((T, wide[k][0]), wide[k][1])
                        for k in ("dh", "first", "dproj", "al", "second", "ul", "gl")})
        scratch.update({"v_cot": V((T, D), BF), "v_dmix": V((T, D), BF), "v_da": V((T, D), F32)})
    if fused:
        scratch["v_bsnd"] = V((T, D), BF)
    scratch.update({"sem_in": pltpu.SemaphoreType.DMA((24,)), "sem_out": pltpu.SemaphoreType.DMA((18, T // TILE)),
                    "sem_mixed": pltpu.SemaphoreType.DMA((1,))})
    names = list(ins) + ["alias_" + k for k in alias] + list(outs) + list(scratch)
    values = [v for v, _ in ins.values()] + [bufs[k] for k in alias]
    results = pl.pallas_call(
        functools.partial(row_kernel, f_rows, b_rows, names),
        out_shape=[o for o, _ in outs.values()],
        in_specs=[m for _, m in ins.values()] + [ANY] * len(alias),
        out_specs=[m for _, m in outs.values()],
        input_output_aliases={len(ins) + i: list(outs).index(k) for i, k in enumerate(alias)},
        scratch_shapes=list(scratch.values()),
        compiler_params=pltpu.CompilerParams(vmem_limit_bytes=58 * 2**20),
        cost_estimate=pl.CostEstimate(flops=8 * 10**9 * does_f + 14 * 10**9 * does_b, bytes_accessed=20 * 2**20,
                                      transcendentals=0),
        name="row_" + "f" * does_f + "b" * does_b,
    )(*values)
    got = dict(zip(outs, results))
    send = (got.get("snd"), got.get("bsnd"))
    if None in send:
        send = send[0] if send[1] is None else send[1]
    return {**bufs, **{k: got[k] for k in keys}}, send, got.get("vec")


def reduce_kernel(n, *refs):
    bits = n.bit_length() - 1
    (gelu_any, gl_any, second_any, ul_any, mixed_any, al_any, first_any, dproj_any, vec_a, vec_b, vec_c, vec_d) = refs[:12]
    (wd_out, wu_out, wo_out, wqkv_out, vec_out) = refs[12:17]
    left, right, total, final, *rest = refs[17:]
    inbox = rest[:bits]
    (vec_box, vec_tmp, sem_load, sem_store, rs_send, rs_recv, ag_send, ag_recv, vec_send, vec_recv) = rest[bits:]
    n_chunks = total.shape[0]
    FF = gelu_any.shape[2]
    D = gl_any.shape[2]
    T = gl_any.shape[1]
    rows = gl_any.shape[0]
    ff_chunks = FF // CHUNK
    me = lax.axis_index("dp")
    size = total.shape[1]
    value = [(me // 2**b) % 2 for b in range(bits)]
    partner = [me + (1 - 2 * value[b]) * 2**b for b in range(bits)]
    base = [sum(value[i] * (size >> (i + 1)) for i in range(b)) for b in range(bits + 1)]

    barrier = pltpu.get_barrier_semaphore()
    for b in range(bits):
        pl.semaphore_signal(barrier, inc=1, device_id={"dp": partner[b]}, device_id_type=MESH)
    pl.semaphore_wait(barrier, bits)

    def halve(c, b):
        half = size >> (b + 1)
        away = pl.multiple_of(base[b] + (1 - value[b]) * half, half)
        return pltpu.make_async_remote_copy(
            src_ref=total.at[c, pl.ds(away, half)], dst_ref=inbox[b].at[c],
            send_sem=rs_send.at[c, b], recv_sem=rs_recv.at[c, b],
            device_id={"dp": partner[b]}, device_id_type=MESH,
        )

    def double(c, b):
        half = size >> (b + 1)
        here = final.at[c, pl.ds(pl.multiple_of(base[b + 1], half), half)]
        return pltpu.make_async_remote_copy(
            src_ref=here, dst_ref=here,
            send_sem=ag_send.at[c, b], recv_sem=ag_recv.at[c, b],
            device_id={"dp": partner[b]}, device_id_type=MESH,
        )

    def add_in(c, b):
        half = size >> (b + 1)
        mine = pl.ds(pl.multiple_of(base[b + 1], half), half)
        target = total if b + 1 < bits else final
        target[c, mine, :] = (total[c, mine, :].astype(F32) + inbox[b][c].astype(F32)).astype(BF)

    def load(c, slot, act):
        def both(a, b):
            for k, (source, target) in enumerate(((a, left), (b, right))):
                act(pltpu.make_async_copy(source, target.at[slot], sem_load.at[k, slot]))

        def cols(ref, j):
            return ref.at[:, :, pl.ds(pl.multiple_of(j * CHUNK, CHUNK), CHUNK)]

        @pl.when(c < ff_chunks)
        def _():
            both(cols(gelu_any, c), gl_any)

        @pl.when((c >= ff_chunks) & (c < 2 * ff_chunks))
        def _():
            both(second_any, cols(ul_any, c - ff_chunks))

        @pl.when(c == 2 * ff_chunks)
        def _():
            both(mixed_any, al_any)

        @pl.when((c > 2 * ff_chunks) & (c < n_chunks))
        def _():
            both(first_any, cols(dproj_any, c - 2 * ff_chunks - 1))

    def store(c, act):
        def block(target):
            act(pltpu.make_async_copy(final.at[c], target, sem_store.at[c]))

        def cols(ref, j):
            return ref.at[:, pl.ds(pl.multiple_of(j * CHUNK, CHUNK), CHUNK)]

        @pl.when((c >= 0) & (c < ff_chunks))
        def _():
            block(wd_out.at[pl.ds(pl.multiple_of(c * CHUNK, CHUNK), CHUNK)])

        @pl.when((c >= ff_chunks) & (c < 2 * ff_chunks))
        def _():
            block(cols(wu_out, c - ff_chunks))

        @pl.when(c == 2 * ff_chunks)
        def _():
            block(wo_out)

        @pl.when(c > 2 * ff_chunks)
        def _():
            block(cols(wqkv_out, c - 2 * ff_chunks - 1))

    def vec_copy(b):
        return pltpu.make_async_remote_copy(
            src_ref=vec_tmp.at[b], dst_ref=vec_box.at[b],
            send_sem=vec_send.at[b], recv_sem=vec_recv.at[b],
            device_id={"dp": partner[b]}, device_id_type=MESH,
        )

    vec_tmp[0] = vec_a[...] + vec_b[...] + vec_c[...] + vec_d[...]
    vec_copy(0).start()
    load(jnp.int32(0), 0, lambda c: c.start())

    gaps = [1, 2] + [1 + b % 2 for b in range(2, bits)]
    lags = [0]
    for gap in gaps[:bits] + gaps[bits - 1::-1]:
        lags.append(lags[-1] + gap)

    def slot_step(t, carry):
        def stage_of(lag, act):
            c = t - lag

            @pl.when((c >= 0) & (c < n_chunks))
            def _():
                act(c)

        def make(c):
            slot = lax.rem(c, 2)
            load(c + 1, 1 - slot, lambda d: d.start())
            load(c, slot, lambda d: d.wait())
            a = left[slot].reshape(rows * T, CHUNK)
            b = right[slot].reshape(rows * T, CHUNK)
            total[c] = dot_tn(a, b).astype(BF)
            halve(c, 0).start()

        def reduce_step(b):
            def act(c):
                halve(c, b).wait()
                add_in(c, b)
                if b + 1 < bits:
                    halve(c, b + 1).start()
                else:
                    double(c, b).start()
            return act

        def gather_step(b):
            def act(c):
                double(c, b).wait()
                double(c, b - 1).start()
            return act

        def finish(c):
            double(c, 0).wait()
            store(c, lambda d: d.start())

        acts = [make] + [reduce_step(b) for b in range(bits)] + [gather_step(b) for b in range(bits - 1, 0, -1)] + [finish]
        for lag, act in zip(lags, acts):
            stage_of(lag, act)
        return carry

    lax.fori_loop(0, n_chunks + lags[-1], slot_step, 0)
    for b in range(bits):
        vec_copy(b).wait()
        merged = vec_tmp[b] + vec_box[b]
        if b + 1 < bits:
            vec_tmp[b + 1] = merged
            vec_copy(b + 1).start()
        else:
            vec_out[...] = merged
    for c in range(n_chunks):
        store(jnp.int32(c), lambda d: d.wait())


def weight_grads(n, bufs, vecs):
    gl, ul = bufs["gl"], bufs["ul"]
    rows, T, D = gl.shape
    FF = ul.shape[2]
    bits = n.bit_length() - 1
    n_chunks = 2 * (FF // CHUNK) + 1 + 3 * D // CHUNK
    size = CHUNK
    S, V, DMA = jax.ShapeDtypeStruct, pltpu.VMEM, pltpu.SemaphoreType.DMA
    return pl.pallas_call(
        functools.partial(reduce_kernel, n),
        out_shape=[S((FF, D), BF), S((D, FF), BF), S((D, D), BF), S((D, 3 * D), BF), S((16, CHUNK), F32)],
        in_specs=[ANY] * 8 + [VMEM] * 4,
        out_specs=[ANY] * 4 + [VMEM],
        scratch_shapes=[
            V((2, rows, T, CHUNK), BF), V((2, rows, T, CHUNK), BF), V((n_chunks, size, CHUNK), BF),
            V((n_chunks, size, CHUNK), BF),
            *[V((n_chunks, size >> (b + 1), CHUNK), BF) for b in range(bits)],
            V((bits, 16, CHUNK), F32), V((bits, 16, CHUNK), F32),
            DMA((2, 2)), DMA((n_chunks,)), DMA((n_chunks, bits)), DMA((n_chunks, bits)), DMA((n_chunks, bits)),
            DMA((n_chunks, bits)), DMA((bits,)), DMA((bits,)),
        ],
        compiler_params=pltpu.CompilerParams(vmem_limit_bytes=52 * 2**20, collective_id=0, has_side_effects=True),
        cost_estimate=pl.CostEstimate(flops=13 * 10**9, bytes_accessed=60 * 2**20, transcendentals=0),
        name="weight_grads",
    )(*[bufs[k] for k in ("gelu", "gl", "second", "ul", "mixed", "al", "first", "dproj")], *vecs)


def body(inputs, cotangent, lengths, norm1_gain, norm1_bias, weight_qkv, weight_out, bias_out, norm2_gain, norm2_bias,
         weight_up, bias_up, weight_down, bias_down):
    w = dict(n1g=norm1_gain, n1b=norm1_bias, wqkv=weight_qkv[0], wo=weight_out[0], bo=bias_out, n2g=norm2_gain,
             n2b=norm2_bias, wu=weight_up[0], bu=bias_up, wd=weight_down[0], bd=bias_down)
    x, cot = inputs[0], cotangent[0]
    n = lax.axis_size("dp")

    def ahead(block):
        return lax.ppermute(block, "section", [(0, 1)])

    def back(block):
        return lax.ppermute(block, "section", [(1, 0)])

    bufs, send_a, _ = row_slot((0, NONE), (NONE, NONE), lengths, x, cot, None, None, w, {})
    row_0 = ahead(send_a)
    bufs, (send_b, back_b), vec_b = row_slot((1, 0), (NONE, 0), lengths, x, cot, row_0, None, w, bufs)
    row_1 = ahead(send_b)
    ret_0 = back(back_b)
    bufs, back_d, vec_d = row_slot((NONE, 1), (NONE, 1), lengths, x, cot, row_1, None, w, bufs)
    ret_1 = back(back_d)
    bufs, _, vec_e = row_slot((NONE, NONE), (0, NONE), lengths, x, cot, None, ret_0, w, bufs)
    bufs, _, vec_g = row_slot((NONE, NONE), (1, NONE), lengths, x, cot, None, ret_1, w, bufs)
    wd, wu, wo, wqkv, vec = weight_grads(n, bufs, (vec_b, vec_d, vec_e, vec_g))

    def wide(v):
        return v.astype(F32)[None]

    return (bufs["out"][None], bufs["dh"][None], vec[0:1], vec[1:2], wide(wqkv), wide(wo), vec[2:3], vec[3:4], vec[4:5],
            wide(wu), vec[6:10].reshape(1, -1), wide(wd), vec[5:6])


def solution(mesh):
    matrix, row = P("section", None, None), P("section", None)
    data = P("section", "dp", None, None)
    return jax.shard_map(
        body,
        mesh=mesh,
        in_specs=(data, data, P("dp", None), row, row, matrix, matrix, row, row, row, matrix, row, matrix, row),
        out_specs=(data, data, row, row, matrix, matrix, row, row, row, matrix, row, matrix, row),
        check_vma=False,
    )
```

time: 377 us -> 349 us (0.926); the launches traced: 376 us -> 343 us
  waiting for transfers between devices: 104 us -> 73.9 us
  Pallas kernels: 245 us -> 223 us
  starting transfers between devices: 9.16 us -> 30.9 us
    ppermute x2, waiting for transfers between devices: 64.9 us -> 33 us  [back(): return lax.ppermute(block, 'section', [(1, 0)])]
    ppermute x2, starting transfers between devices: 6.58 us -> 28.3 us  [ahead(): return lax.ppermute(block, 'section', [(0, 1)])]
    pallas_call x6 -> x5, Pallas kernels: 135 us -> 123 us  [row_slot(): pl.pallas_call(functools.partial(row_kernel, f_rows, b_rows, names), out_...]
    pallas_call x1, Pallas kernels: 110 us -> 100 us  [weight_grads(): pl.pallas_call(functools.partial(reduce_kernel, n), out_shape=[S((FF, D),...]
  transfers between devices with their start and end apart: 4 -> 4, of which waited for: 4 -> 3; matrix products, arithmetic and copies ran while one was open for 0% -> 0% of each run, Pallas kernels for 1% -> 13%
where the time goes in v2:
time: 349 us; the launch traced here: 343 us
  Pallas kernels  223 us (64%)
  waiting for transfers between devices  73.9 us (21%)
  starting transfers between devices  30.9 us (9%)
  other arithmetic  8.32 us (2%)
  local copies, waits for them, and re-layouts  5.9 us (2%)
    pallas_call x5, Pallas kernels, row_slot(): pl.pallas_call(functools.partial(row_kernel, f_rows, b_rows, names), out_...  123 us
    pallas_call x1, Pallas kernels, weight_grads(): pl.pallas_call(functools.partial(reduce_kernel, n), out_shape=[S((FF, D),...  100 us
    ppermute x2, waiting for transfers between devices, ahead(): return lax.ppermute(block, 'section', [(0, 1)])  41 us
    ppermute x2, waiting for transfers between devices, back(): return lax.ppermute(block, 'section', [(1, 0)])  33 us
    ppermute x2, starting transfers between devices, ahead(): return lax.ppermute(block, 'section', [(0, 1)])  28.3 us
    broadcast_in_dim x4, other arithmetic, wide(): return v.astype(F32)[None]  8.32 us
  transfers between devices with their start and end apart: 4, of which 3 were waited for; matrix products, arithmetic and copies ran while one was open for 0% of the time, Pallas kernels for 13%

profile of v2, /device:TPU:0, one launch (start us, length us, event | category | flops | bytes accessed | tf_op | source)
XLA Modules:
  0.0 343.3 jit_solution(3690876119416669388)
XLA Ops:
  0.6 21.3 %row_f.1 = (bf16[2,1024,512]{2,1,0:T(8,128)(2,1)}, bf16[2,1024,512]{2,1,0:T(8,128)(2,1)}, bf16[2,1024,1536]{2,1,0:T(8,128)(2,1)}, f32[2,1024,512]{2,1,0:T(8,128)...) custom-call(s32[2,8]{1,0:T(2,128)} %refs_0_.9, bf16[2,1024,512]{2,1,0:T(8,128)(2,1)} %bitcast.25, ...), custom_call_target="tpu_custom_call" | custom-call | flops 8000000000 | bytes 20971520 | tf_op jit(solution)/shard_map/row_f/pallas_call | solution.py:486
  22.0 1.4 collective-permute-start
  23.3 22.8 %collective-permute-done.refs_3_ = bf16[1024,512]{1,0:T(8,128)(2,1)S(1)} collective-permute-done((bf16[1024,512]{1,0:T(8,128)(2,1)}, bf16[1024,512]{1,0:T(8,128)(2,1)S(1)}, u32[]{:S(2)}, u32[]{:S(2)}) %collective-permute-start) | collective-permute-done | bytes 1048608 | tf_op jit(solution)/shard_map/ppermute | solution.py:706
  46.1 0.0 copy-start.10
  46.1 1.0 copy-done.10
  47.1 26.0 %row_fb.2 = (bf16[2,1024,512]{2,1,0:T(8,128)(2,1)}, bf16[2,1024,512]{2,1,0:T(8,128)(2,1)}, bf16[2,1024,1536]{2,1,0:T(8,128)(2,1)}, f32[2,1024,512]{2,1,0:T(8,128...) custom-call(s32[2,8]{1,0:T(2,128)} %refs_0_.9, ...), custom_call_target="tpu_custom_call", output_to_operand_aliasing={{0}: (15, {}), {1}: (16, {}), {2}: (17, {}), {3}: (18, {}),... | custom-call | flops 22000001024 | bytes 20971520 | tf_op jit(solution)/shard_map/row_fb/pallas_call | solution.py:486
  73.1 27.0 %collective-permute-start.1 = (bf16[1024,512]{1,0:T(8,128)(2,1)}, bf16[1024,512]{1,0:T(8,128)(2,1)S(1)}, u32[]{:S(2)}, u32[]{:S(2)}) collective-permute-start(bf16[1024,512]{1,0:T(8,128)(2,1)} %get-tuple-element.76), channel_id=1, source_target_pairs={{0,16},{1,17},{2,18},{3,19},{4,20},{5,21},{6,22},{7,23},{8,24},{9,... | collective-permute-start | bytes 3145736 | tf_op jit(solution)/shard_map/ppermute | solution.py:706
  100.1 1.3 collective-permute-start.3
  101.4 18.2 %collective-permute-done.1.refs_3_ = bf16[1024,512]{1,0:T(8,128)(2,1)S(1)} collective-permute-done((bf16[1024,512]{1,0:T(8,128)(2,1)}, bf16[1024,512]{1,0:T(8,128)(2,1)S(1)}, u32[]{:S(2)}, u32[]{:S(2)}) %collective-permute-start.1) | collective-permute-done | bytes 1048608 | tf_op jit(solution)/shard_map/ppermute | solution.py:706
  119.5 0.0 copy-start.9
  119.5 1.0 copy-done.9
  120.5 9.8 %row_fb.3 = (bf16[2,1024,512]{2,1,0:T(8,128)(2,1)}, bf16[2,1024,512]{2,1,0:T(8,128)(2,1)}, f32[2,1024,512]{2,1,0:T(8,128)}, bf16[2,1024,512]{2,1,0:T(8,128)(2,1)...) custom-call(s32[2,8]{1,0:T(2,128)} %refs_0_.9, ...), custom_call_target="tpu_custom_call", output_to_operand_aliasing={{0}: (15, {}), {1}: (16, {}), {2}: (17, {}), {3}: (18, {}),... | custom-call | flops 22000001024 | bytes 20971520 | tf_op jit(solution)/shard_map/row_fb/pallas_call | solution.py:486
  130.3 1.3 collective-permute-start.2
  131.6 0.0 collective-permute-done.3.refs_3_
  131.6 0.0 copy-start.7
  131.6 1.0 copy-done.7
  132.6 33.2 %row_b.2 = (f32[2,1024,512]{2,1,0:T(8,128)}, bf16[2,1024,512]{2,1,0:T(8,128)(2,1)}, bf16[2,1024,1536]{2,1,0:T(8,128)(2,1)}, bf16[2,1024,512]{2,1,0:T(8,128)(2,1)...) custom-call(s32[2,8]{1,0:T(2,128)} %refs_0_.9, ...), custom_call_target="tpu_custom_call", output_to_operand_aliasing={{0}: (18, {}), {1}: (19, {}), {2}: (20, {}), {3}: (21, {}),... | custom-call | flops 14000000000 | bytes 20971520 | tf_op jit(solution)/shard_map/row_b/pallas_call | solution.py:486
  165.7 33.0 %collective-permute-done.2.refs_3_ = bf16[1024,512]{1,0:T(8,128)(2,1)S(1)} collective-permute-done((bf16[1024,512]{1,0:T(8,128)(2,1)}, bf16[1024,512]{1,0:T(8,128)(2,1)S(1)}, u32[]{:S(2)}, u32[]{:S(2)}) %collective-permute-start.2) | collective-permute-done | bytes 1048608 | tf_op jit(solution)/shard_map/ppermute | solution.py:709
  198.7 0.0 copy-start.8
  198.7 1.0 copy-done.8
  199.7 0.0 copy-start
  199.7 0.0 copy-start.2
  199.7 0.0 copy-start.3
  199.7 32.7 %row_b.3 = (f32[2,1024,512]{2,1,0:T(8,128)}, bf16[2,1024,512]{2,1,0:T(8,128)(2,1)}, bf16[2,1024,1536]{2,1,0:T(8,128)(2,1)}, bf16[2,1024,512]{2,1,0:T(8,128)(2,1)...) custom-call(s32[2,8]{1,0:T(2,128)} %refs_0_.9, ...), custom_call_target="tpu_custom_call", output_to_operand_aliasing={{0}: (18, {}), {1}: (19, {}), {2}: (20, {}), {3}: (21, {}),... | custom-call | flops 14000000000 | bytes 20971520 | tf_op jit(solution)/shard_map/row_b/pallas_call | solution.py:486
  232.4 0.0 copy-done
  232.4 0.0 copy-done.2
  232.4 0.0 copy-done.3
  232.4 0.0 copy-start.1
  232.4 0.7 copy-done.1
  233.1 100.3 %weight_grads.1 = (bf16[2048,512]{1,0:T(8,128)(2,1)}, bf16[512,2048]{1,0:T(8,128)(2,1)}, bf16[512,512]{1,0:T(8,128)(2,1)S(1)}, bf16[512,1536]{1,0:T(8,128)(2,1)}, f32[16,512]{1,0:T(8,128)S(1)}) custom-call(bf16[2,1024,2048]{2,1,0:T(8,128)(2,1)} %get-tuple-element.110.refs_0_, bf16[2,1024,512]{2,1,0:T(8,128)(2,1)} %get-tuple-element.111.refs_1_, ...), custom_call_target="tpu_custom_call" | custom-call | flops 12999999488 | bytes 62914560 | tf_op jit(solution)/shard_map/weight_grads/pallas_call | solution.py:679
  333.5 0.0 copy-start.6
  333.5 0.6 fusion
  334.1 0.6 copy.58
  334.7 1.1 bitcast_convert_fusion.3
  335.8 0.0 copy-done.6
  335.8 0.0 copy-start.5
  335.8 2.1 bitcast_convert_fusion.2
  337.9 0.0 copy-done.5
  337.9 0.0 copy-start.4
  337.9 2.5 bitcast_convert_fusion.1
  340.5 0.0 copy-done.4
  340.5 2.6 bitcast_convert_fusion
  (1 shorter events, 0.0 us)
Async XLA Ops:
  22.0 24.2 %collective-permute-start = (bf16[1024,512]{1,0:T(8,128)(2,1)}, bf16[1024,512]{1,0:T(8,128)(2,1)S(1)}, u32[]{:S(2)}, u32[]{:S(2)}) collective-permute-start(bf16[1024,512]{1,0:T(8,128)(2,1)} %get-tuple-element.70), channel_id=1, source_target_pairs={{0,16},{1,17},{2,18},{3,19},{4,20},{5,21},{6,22},{7,23},{8,24},{9,... | collective-permute-start | bytes 3145736 | tf_op jit(solution)/shard_map/ppermute | solution.py:706
  46.1 1.0 copy-start.10
  73.1 46.4 %collective-permute-start.1 = (bf16[1024,512]{1,0:T(8,128)(2,1)}, bf16[1024,512]{1,0:T(8,128)(2,1)S(1)}, u32[]{:S(2)}, u32[]{:S(2)}) collective-permute-start(bf16[1024,512]{1,0:T(8,128)(2,1)} %get-tuple-element.76), channel_id=1, source_target_pairs={{0,16},{1,17},{2,18},{3,19},{4,20},{5,21},{6,22},{7,23},{8,24},{9,... | collective-permute-start | bytes 3145736 | tf_op jit(solution)/shard_map/ppermute | solution.py:706
  100.1 31.5 %collective-permute-start.3 = (bf16[1024,512]{1,0:T(8,128)(2,1)}, bf16[1024,512]{1,0:T(8,128)(2,1)S(1)}, u32[]{:S(2)}, u32[]{:S(2)}) collective-permute-start(bf16[1024,512]{1,0:T(8,128)(2,1)} %get-tuple-element.92), channel_id=1, source_target_pairs={{16,0},{17,1},{18,2},{19,3},{20,4},{21,5},{22,6},{23,7},{24,8},{25... | collective-permute-start | bytes 3145736 | tf_op jit(solution)/shard_map/ppermute | solution.py:709
  119.5 1.0 copy-start.9
  130.3 68.4 %collective-permute-start.2 = (bf16[1024,512]{1,0:T(8,128)(2,1)}, bf16[1024,512]{1,0:T(8,128)(2,1)S(1)}, u32[]{:S(2)}, u32[]{:S(2)}) collective-permute-start(bf16[1024,512]{1,0:T(8,128)(2,1)} %get-tuple-element.88), channel_id=1, source_target_pairs={{16,0},{17,1},{18,2},{19,3},{20,4},{21,5},{22,6},{23,7},{24,8},{25... | collective-permute-start | bytes 3145736 | tf_op jit(solution)/shard_map/ppermute | solution.py:709
  131.6 1.0 copy-start.7
  198.7 1.0 copy-start.8
  199.7 32.7 %copy-start = (f32[16,512]{1,0:T(8,128)S(1)}, f32[16,512]{1,0:T(8,128)}, u32[]{:S(2)}) copy-start(f32[16,512]{1,0:T(8,128)} %get-tuple-element.120.refs_10_) | copy-start | bytes 98308
  199.7 32.7 %copy-start.2 = (f32[16,512]{1,0:T(8,128)S(1)}, f32[16,512]{1,0:T(8,128)}, u32[]{:S(2)}) copy-start(f32[16,512]{1,0:T(8,128)} %get-tuple-element.118.refs_8_) | copy-start | bytes 98308
  199.7 32.7 %copy-start.3 = (f32[16,512]{1,0:T(8,128)S(1)}, f32[16,512]{1,0:T(8,128)}, u32[]{:S(2)}) copy-start(f32[16,512]{1,0:T(8,128)} %get-tuple-element.119.refs_9_) | copy-start | bytes 98308
  232.4 0.8 copy-start.1
  333.5 2.3 copy-start.6
  335.8 2.1 copy-start.5
  337.9 2.5 copy-start.4
